TPU v7x, 128 devices: a whole 4x4x4 slice. The times are simulated.
128 devices in a mesh: row: 8 (over x, y_lo), col: 16 (over y_hi, z, core).
Axes of the slice: x: 4, y: 4 (y_hi: 2, y_lo: 2; y = y_hi * 2 + y_lo), z: 4, core: 2. Of those that a mesh axis runs over, the one named last changes fastest.
Arguments:
- momentum: float32 [29568, 8192], P(('row', 'col')), may hold values from -100 to 100
- gradient: bfloat16 [29568, 8192], P(('row', 'col')), may hold values from -24 to 24
- right_basis: bfloat16 [8192, 512], P(('row', 'col')), may hold values from -0.0625 to 0.0625
- weight: bfloat16 [29568, 8192], P('row', 'col'), may hold values from -6 to 6
- tokens: bfloat16 [512, 29568], P('col', 'row'), may hold values from -6 to 6
Outputs:
- new_momentum: float32 [29568, 8192], P(('row', 'col'))
- new_basis: bfloat16 [8192, 512], P(('row', 'col'))
- new_weight: bfloat16 [29568, 8192], P('row', 'col')
- logits: bfloat16 [512, 8192], P('row', 'col')
All inputs are finite; a program needn't handle non-finite values.
Results may differ from a plain program's by a relative error of at most 0.02.
Values may be sent and summed in bfloat16 or wider, within the bound.
No kernel may reach another device: no remote copies, remote signals or barrier semaphores. Data moves between devices by JAX's collectives and lax.ppermute only.
A program may use at most 128 MiB of HBM per device.

v0:
```python
import math

import jax
import jax.numpy as jnp
from jax import lax
from jax.experimental import pallas as pl
from jax.experimental.pallas import tpu as pltpu
from jax.sharding import PartitionSpec as P

EPSILON = 1e-06
MOMENTUM_DECAY = 0.95
STEP_SIZE = 0.3
BF = jnp.bfloat16
F32 = jnp.float32
ALL = ("row", "col")
VMEM_LIMIT = 48 * 1024 * 1024
HALF = 256
TALL = HALF + 32
UNIT = 512


def device_id(x, y, z, core):
    x, y, z = x % 4, y % 4, z % 4
    return (x * 2 + y % 2) * 16 + (y // 2) * 8 + z * 2 + core


def places():
    return [(x, y, z, c) for x in range(4) for y in range(4) for z in range(4) for c in range(2)]


def moved(place, axis, shift):
    place = list(place)
    place["xyz".index(axis)] += shift
    return device_id(*place)


def shift_by(value, axes, shift):
    pairs = [(device_id(*p), moved(p, axes[p[3]], shift)) for p in places()]
    return lax.ppermute(value, ALL, pairs)


def gather_z(value):
    groups = [[y * 8 + z * 2 + c for z in range(4)] for y in range(2) for c in range(2)]
    return lax.all_gather(value, "col", axis=0, axis_index_groups=groups, tiled=True)


def exchange(value, axis, distance):
    pairs = []
    for p in places():
        other = list(p)
        other["xyz".index(axis)] ^= distance
        pairs.append((device_id(*p), device_id(*other)))
    return lax.ppermute(value, ALL, pairs)


def swap_y_lo(value):
    return exchange(value, "y", 1)


def swap_cores(value):
    return lax.ppermute(value, ALL, [(i, i ^ 1) for i in range(128)])


def gather_ring(block, axes, far_block=None):
    ahead = shift_by(block, axes, -1)
    before = shift_by(block, axes, 1)
    across = shift_by(block if far_block is None else far_block, axes, 2)
    return [block, ahead, across, before]


def scatter_ring(blocks, axes, done=None):
    from_before = shift_by(blocks[1], axes, 1)
    from_after = shift_by(blocks[3], axes, -1)
    from_across = shift_by(blocks[2], axes, 2)
    if done is not None:
        from_across = after(from_across, *done)
    return (
        (blocks[0].astype(F32) + from_across.astype(F32))
        + (from_before.astype(F32) + from_after.astype(F32))
    )


def rotate(stack, start):
    return lax.dynamic_slice_in_dim(jnp.concatenate([stack, stack], 0), start, 4, 0)


def after(value, *done):
    return lax.optimization_barrier((value, *done))[0]


def params():
    return pltpu.CompilerParams(vmem_limit_bytes=VMEM_LIMIT)


def column_specs(rows, count):
    return [
        pl.BlockSpec((rows, UNIT), lambda i, order, u=u: (0, order[4 * i + u])) for u in range(count)
    ]


def project(order, own, other, pieces, sums=None, tokens=()):
    rows = own.shape[0]
    count = len(pieces)
    last = sums is not None

    def kernel(order_ref, *refs):
        own_refs, other_refs, slabs = refs[:4], refs[4:8], refs[8 : 8 + count]
        rest = refs[8 + count :]
        step = pl.program_id(0)

        def part(columns, slab):
            total = jnp.dot(columns[0][...], slab[0], preferred_element_type=F32)
            for u in range(1, 4):
                total += jnp.dot(columns[u][...], slab[u], preferred_element_type=F32)
            return total

        if last:
            mine = rest[0][...] + part(own_refs, slabs[0])
            theirs = rest[1][...] + part(other_refs, slabs[0])
            rest[4][...] = mine
            rest[5][...] = mine.astype(BF)
            rest[6][...] = theirs.astype(BF)
            squares = jnp.sum(mine * mine + theirs * theirs, axis=0, keepdims=True)
            low, high = (jnp.concatenate([squares[:, at : at + 128]] * 4, 1) for at in (0, 128))
            line = lax.broadcasted_iota(jnp.int32, (16, UNIT), 0)
            squares = jnp.where(line == 0, low, jnp.where(line == 1, high, 0.0)).astype(BF)
            product = jnp.dot(rest[2][...], rest[5][...], preferred_element_type=F32)
            product += jnp.dot(rest[3][...], rest[6][...], preferred_element_type=F32)
            for u in range(16):
                eight = [product[at : at + 8] for at in range(32 * u, 32 * u + 32, 8)]
                eight = [jnp.concatenate([e[:, :128], e[:, 128:]], 0) for e in eight]
                rest[7][u, :16] = squares
                rest[7][u, 16:] = jnp.concatenate(eight, 1).astype(BF)
            return
        for k, slab in enumerate(slabs):

            @pl.when(step == k)
            def _(slab=slab, k=k):
                mine, theirs = part(own_refs, slab), part(other_refs, slab)
                rest[0][...] = mine if k == 0 else rest[0][...] + mine
                rest[1][...] = theirs if k == 0 else rest[1][...] + theirs

    whole = pl.BlockSpec((rows, HALF), lambda i, order: (0, 0))
    slab_spec = pl.BlockSpec((4, UNIT, HALF), lambda i, order: (0, 0, 0))
    shape = lambda dtype: jax.ShapeDtypeStruct((rows, HALF), dtype)
    in_specs = column_specs(rows, 4) * 2 + [slab_spec] * count
    out_specs, out_shape = [whole, whole], [shape(F32), shape(F32)]
    if last:
        in_specs += [whole, whole] + [pl.BlockSpec(t.shape, lambda i, order: (0, 0)) for t in tokens]
        out_specs = [whole, whole, whole, pl.BlockSpec((16, 32, UNIT), lambda i, order: (0, 0, 0))]
        out_shape = [shape(F32), shape(BF), shape(BF), jax.ShapeDtypeStruct((16, 32, UNIT), BF)]
    return pl.pallas_call(
        kernel,
        grid_spec=pltpu.PrefetchScalarGridSpec(
            num_scalar_prefetch=1, grid=(count,), in_specs=in_specs, out_specs=out_specs
        ),
        out_shape=out_shape,
        compiler_params=params(),
    )(order, *([own] * 4), *([other] * 4), *pieces, *(sums or ()), *tokens)


def project_back(order, own, other, p_own, p_other, below):
    rows = own.shape[0]
    count = order.shape[0] // 4
    contract = (((0,), (0,)), ((), ()))

    def kernel(order_ref, *refs):
        own_refs, other_refs, below_refs, outs = refs[:4], refs[4:8], refs[10:14], refs[14:]
        p_own_ref, p_other_ref = refs[8:10]
        step = pl.program_id(0)
        for k, out in enumerate(outs):

            @pl.when(step == k)
            def _(out=out):
                for u in range(4):
                    value = lax.dot_general(
                        p_own_ref[...], own_refs[u][...], contract, preferred_element_type=F32
                    )
                    value += lax.dot_general(
                        p_other_ref[...], other_refs[u][...], contract, preferred_element_type=F32
                    )
                    out[u, :HALF] = value.astype(BF)
                    out[u, HALF:] = below_refs[u][0]

    whole = pl.BlockSpec((rows, HALF), lambda i, order: (0, 0))
    return pl.pallas_call(
        kernel,
        grid_spec=pltpu.PrefetchScalarGridSpec(
            num_scalar_prefetch=1,
            grid=(count,),
            in_specs=column_specs(rows, 4) * 2
            + [whole, whole]
            + [
                pl.BlockSpec((1, 32, UNIT), lambda i, order, u=u: (order[4 * i + u], 0, 0))
                for u in range(4)
            ],
            out_specs=[pl.BlockSpec((4, TALL, UNIT), lambda i, order: (0, 0, 0))] * count,
        ),
        out_shape=[jax.ShapeDtypeStruct((4, TALL, UNIT), BF)] * count,
        compiler_params=params(),
    )(order, *([own] * 4), *([other] * 4), p_own, p_other, *([below] * 4))


def update_momentum(order, units, momentum, gradient, left_own, left_other, q_own, q_other, tile=None):
    rows, width = momentum.shape
    count = len(units)
    own = sorted({k for k, _ in units})
    other = sorted({j for _, j in units})
    chunks = 3

    def kernel(order_ref, lo_ref, lp_ref, m_ref, g_ref, *refs):
        own_refs = dict(zip(own, refs))
        other_refs = dict(zip(other, refs[len(own) :]))
        refs = refs[len(own) + len(other) :]
        if tile is not None:
            _, place_ref, f_ref, *small_refs, w_ref, po_ref, pp_ref = refs[:9]
            new_ref, logits_ref, basis_ref = refs[10:13]
            (early_ref, mine_ref, theirs_ref), refs_left = refs[-4:-1], refs[:-4]
            small_sems = refs[-1]
            w_all, po_all, pp_all, w_out, unit, scaled, lines, w_sems, unit_sems, w_out_sems = refs_left[-10:]
            out_ref, refs = refs[9], refs_left[13:-10]
        else:
            out_ref, refs = refs[0], refs[1:]
        m_all, g_all, qo_all, qp_all, out_all, in_sems, out_sems = refs
        loads, stores = [], []
        for n, (k, j) in enumerate(units):
            columns = pl.ds(pl.multiple_of(order_ref[n] * UNIT, UNIT), UNIT)
            pairs = (
                (m_ref.at[:, columns], m_all.at[n]),
                (g_ref.at[:, columns], g_all.at[n]),
                (own_refs[k].at[j, pl.ds(0, HALF)], qo_all.at[n]),
                (other_refs[j].at[k, pl.ds(0, HALF)], qp_all.at[n]),
            )
            loads.append(
                [pltpu.make_async_copy(a, b, in_sems.at[n, i]) for i, (a, b) in enumerate(pairs)]
            )
            stores.append(pltpu.make_async_copy(out_all.at[n], out_ref.at[:, columns], out_sems.at[n]))
        for copies in loads:
            for copy in copies:
                copy.start()
        if tile is not None:
            small = [
                pltpu.make_async_copy(a, b, small_sems.at[n])
                for n, (a, b) in enumerate(zip(small_refs, (early_ref, mine_ref, theirs_ref)))
            ]
            for copy in small:
                copy.start()
            wanted = []
            for side, (slabs, far, near) in enumerate(((own_refs, 0, 1), (other_refs, 1, 0))):
                wanted.append(
                    [
                        (0, pl.ds(0, HALF), unit.at[side]),
                        (2, pl.ds(HALF + 16, 16), lines.at[side, 0]),
                        (4, pl.ds(HALF + 16, 16), lines.at[side, 1]),
                    ]
                )
                for n, (at, part, target) in enumerate(wanted[side]):
                    for k in range(4):

                        @pl.when(place_ref[at + far] == k)
                        def _(slabs=slabs, side=side, n=n, at=at, near=near, part=part, target=target, k=k):
                            source = slabs[k].at[place_ref[at + near], part]
                            pltpu.make_async_copy(source, target, unit_sems.at[side, n]).start()

            chunk = w_ref.shape[0] // chunks
            parts = [pl.ds(i * chunk, chunk) for i in range(chunks)]
            w_loads = [
                [
                    pltpu.make_async_copy(a.at[part], b.at[part], w_sems.at[i, n])
                    for n, (a, b) in enumerate(((w_ref, w_all), (po_ref, po_all), (pp_ref, pp_all)))
                ]
                for i, part in enumerate(parts)
            ]
            w_stores = [
                pltpu.make_async_copy(w_out.at[part], new_ref.at[part], w_out_sems.at[i])
                for i, part in enumerate(parts)
            ]
            for copies in w_loads:
                for copy in copies:
                    copy.start()
        for n in range(count):
            for copy in loads[n]:
                copy.wait()
            change = jnp.dot(lo_ref[...], qo_all[n], preferred_element_type=F32)
            change += jnp.dot(lp_ref[...], qp_all[n], preferred_element_type=F32)
            out_all[n] = (m_all[n] + g_all[n].astype(F32)) - (1.0 - MOMENTUM_DECAY) * change
            stores[n].start()
        if tile is not None:
            for copy in small:
                copy.wait()
            core = pl.multiple_of(place_ref[6] * HALF, HALF)
            basis_ref[:, pl.ds(core, HALF)] = (mine_ref[...].astype(F32) * f_ref[2:3]).astype(BF)
            basis_ref[:, pl.ds(HALF - core, HALF)] = (
                theirs_ref[...].astype(F32) * f_ref[3:4]
            ).astype(BF)
            late = 0.0
            for side in range(2):
                for n, (_, part, target) in enumerate(wanted[side]):
                    pltpu.make_async_copy(own_refs[0].at[0, part], target, unit_sems.at[side, n]).wait()
                factor = jnp.transpose(jnp.broadcast_to(f_ref[side : side + 1], (128, HALF)))
                for at in range(0, UNIT, 128):
                    columns = slice(at, at + 128)
                    scaled[side, :, columns] = (
                        unit[side, :, columns].astype(F32) * factor
                    ).astype(BF)
                product = []
                for half in range(2):
                    block = lines[side, half].astype(F32)
                    for at in range(0, UNIT, 128):
                        eight = block[:, at : at + 128]
                        product.append(jnp.concatenate([eight[:8], eight[8:]], 1))
                product = jnp.concatenate(product, 0).astype(BF)
                late += jnp.dot(product, scaled[side], preferred_element_type=F32)
            logits_ref[...] = ((early_ref[...].astype(F32) - late) * tile[-1]).astype(BF)
            for i, part in enumerate(parts):
                for copy in w_loads[i]:
                    copy.wait()
                change = jnp.dot(po_all[part, :], scaled[0], preferred_element_type=F32)
                change += jnp.dot(pp_all[part, :], scaled[1], preferred_element_type=F32)
                w_out[part, :] = (w_all[part, :].astype(F32) - change).astype(BF)
                w_stores[i].start()
            for copy in w_stores:
                copy.wait()
        for copy in stores:
            copy.wait()

    anywhere = pl.BlockSpec(memory_space=pl.ANY)
    vmem = pl.BlockSpec(memory_space=pltpu.VMEM)
    smem = pl.BlockSpec(memory_space=pltpu.SMEM)
    operands = [order, left_own, left_other, momentum, gradient]
    in_specs = [smem, vmem, vmem, anywhere, anywhere]
    operands += [q_own[k] for k in own] + [q_other[j] for j in other]
    in_specs += [anywhere] * (len(own) + len(other))
    out_specs, out_shape = [anywhere], [jax.ShapeDtypeStruct((rows, width), F32)]
    scratch_shapes = [
        pltpu.VMEM((count, rows, UNIT), F32),
        pltpu.VMEM((count, rows, UNIT), BF),
        pltpu.VMEM((count, HALF, UNIT), BF),
        pltpu.VMEM((count, HALF, UNIT), BF),
        pltpu.VMEM((count, rows, UNIT), F32),
        pltpu.SemaphoreType.DMA((count, 4)),
        pltpu.SemaphoreType.DMA((count,)),
    ]
    aliases = {}
    if tile is not None:
        aliases = {len(operands): 0}
        operands += tile[:-1]
        in_specs += [anywhere, smem, vmem] + [anywhere] * 6
        tall, tokens = tile[6].shape[0], tile[3].shape[0]
        out_specs += [anywhere, vmem, vmem]
        out_shape += [
            jax.ShapeDtypeStruct((tall, UNIT), BF),
            jax.ShapeDtypeStruct((tokens, UNIT), BF),
            jax.ShapeDtypeStruct((tokens, UNIT), BF),
        ]
        scratch_shapes += [
            pltpu.VMEM((tall, UNIT), BF),
            pltpu.VMEM((tall, HALF), BF),
            pltpu.VMEM((tall, HALF), BF),
            pltpu.VMEM((tall, UNIT), BF),
            pltpu.VMEM((2, HALF, UNIT), BF),
            pltpu.VMEM((2, HALF, UNIT), BF),
            pltpu.VMEM((2, 2, 16, UNIT), BF),
            pltpu.SemaphoreType.DMA((chunks, 3)),
            pltpu.SemaphoreType.DMA((2, 3)),
            pltpu.SemaphoreType.DMA((chunks,)),
            pltpu.VMEM((tokens, UNIT), BF),
            pltpu.VMEM((tokens, HALF), BF),
            pltpu.VMEM((tokens, HALF), BF),
            pltpu.SemaphoreType.DMA((3,)),
        ]
    return pl.pallas_call(
        kernel,
        in_specs=in_specs,
        out_specs=out_specs,
        out_shape=out_shape,
        scratch_shapes=scratch_shapes,
        input_output_aliases=aliases,
        compiler_params=params(),
    )(*operands)


def sum_squares(slabs):
    def kernel(*refs):
        total = sum(ref[u].astype(F32) for ref in refs[:4] for u in range(4))
        total = sum(total[:, at : at + 128] for at in range(0, UNIT, 128))
        refs[4][...] = total[0:2] + total[2:4] + total[4:6]

    return pl.pallas_call(
        kernel,
        grid=(1,),
        in_specs=[pl.BlockSpec((4, 16, UNIT), lambda i: (0, HALF // 16, 0))] * 4,
        out_specs=pl.BlockSpec((2, 128), lambda i: (0, 0)),
        out_shape=jax.ShapeDtypeStruct((2, 128), F32),
        compiler_params=params(),
    )(*slabs)


def three_terms(value):
    high = value.astype(BF)
    rest = value - high.astype(F32)
    middle = rest.astype(BF)
    return jnp.stack([high, middle, (rest - middle.astype(F32)).astype(BF)])


def shards(momentum, gradient, right_basis, weight, tokens):
    row, col = lax.axis_index("row"), lax.axis_index("col")
    x, y, z, core = row // 2, (col // 8) * 2 + row % 2, (col // 2) % 4, col % 2
    first = core == 0
    total_rows = momentum.shape[0] * 128
    rank = right_basis.shape[1]
    width = momentum.shape[1]
    rows = momentum.shape[0]
    big, middle = ("x", "y"), ("y", "x")
    deep = ("z", "z")

    def unit_at(k, j):
        ux = jnp.where(first, x + k, x + j) % 4
        uy = jnp.where(first, y + j, y + k) % 4
        return ux * 4 + (uy % 2) * 2 + uy // 2

    def orders(units):
        return jnp.stack([unit_at(k, j) for k, j in units]).astype(jnp.int32)

    def slab_orders(*slabs):
        return orders([(k, j) for k in slabs for j in range(4)])

    def halves(a):
        low, high = a[:, :HALF], a[:, HALF:]
        return jnp.where(first, low, high), jnp.where(first, high, low)

    def by_core(mine, theirs):
        return jnp.where(first, mine, theirs), jnp.where(first, theirs, mine)

    def by_half(mine, theirs):
        low = y < 2
        return jnp.stack([jnp.where(low, mine, theirs), jnp.where(low, theirs, mine)])

    def swap_y_hi(value):
        return shift_by(value, ("y", "y"), 2)

    def pick(bit, values):
        return jnp.where(bit == 0, values[0], values[1]), jnp.where(bit == 0, values[1], values[0])

    basis_own, basis_sent = halves(right_basis)
    basis_other = swap_cores(basis_sent)
    basis_chip = jnp.concatenate(by_core(basis_own, basis_other), 0)
    stack = jnp.stack(gather_ring(basis_chip, deep))
    unit = rotate(stack, (4 - z) % 4).reshape(UNIT, HALF)
    tokens_near = swap_y_hi(tokens)
    unit, tokens_near = lax.optimization_barrier((unit, tokens_near))

    momentum_in, gradient_in, _ = lax.optimization_barrier((momentum, gradient, unit))
    buffer_low = (momentum_in + gradient_in.astype(F32)).astype(BF)
    slab = jnp.stack(gather_ring(unit, middle))
    slab, buffer_sent = lax.optimization_barrier((slab, buffer_low))
    pieces = gather_ring(slab, big)
    buffer_other = swap_cores(buffer_sent)

    tokens_all = lax.all_gather(
        by_half(tokens, tokens_near).reshape(64, -1), "col", axis=0,
        axis_index_groups=[[8 * k + i for i in range(8)] for k in range(2)], tiled=True,
    )
    token_parts = [
        lax.dynamic_slice_in_dim(tokens_all, rows * c, rows, 1) for c in (col, col ^ 1)
    ]

    early = jnp.dot(tokens_all, weight, preferred_element_type=F32).astype(BF)
    early = early.reshape(4, 2, 2, 32, -1).transpose(2, 0, 1, 3, 4).reshape(2, 2, 2, 64, -1)
    pieces[3], early, *token_parts = lax.optimization_barrier((pieces[3], early, *token_parts))

    def halve(value, bit, send):
        kept, sent = pick(bit, value)
        return (kept.astype(F32) + send(sent).astype(F32)).astype(BF)

    sums = project(slab_orders(0, 1, 3), buffer_low, buffer_other, [pieces[0], pieces[1], pieces[3]])
    p_own, p_own_low, p_other, below = project(
        slab_orders(2), buffer_low, buffer_other, [pieces[2]], sums, token_parts
    )

    slabs = [None] * 4
    (slabs[2],) = project_back(slab_orders(2), buffer_low, buffer_other, p_own_low, p_other, below)
    slabs[1], slabs[3] = project_back(
        slab_orders(1, 3), buffer_low, buffer_other, p_own_low, p_other, below
    )
    (slabs[0],) = project_back(slab_orders(0), buffer_low, buffer_other, p_own_low, p_other, below)
    early, p_own_sent, p_other_sent, _ = lax.optimization_barrier(
        (early, p_own_low, p_other, slabs[2])
    )
    early = halve((early[:, :, 0], early[:, :, 1]), row % 2, swap_y_lo)
    p_chip = jnp.stack(by_core(p_own_sent, p_other_sent))
    p_pair = by_half(p_chip, swap_y_hi(p_chip))
    summed = scatter_ring(slabs, big, (early, p_pair)).astype(BF)
    p_tile = gather_z(p_pair[None])
    early = halve((early[:, 0], early[:, 1]), x % 2, lambda v: exchange(after(v, summed), "x", 1))
    summed = scatter_ring([summed[k] for k in range(4)], middle, (early,)).astype(BF)
    early = halve((early[0], early[1]), x // 2, lambda v: exchange(after(v, summed), "x", 2))
    summed = summed.reshape(TALL, 4, 128).transpose(1, 0, 2)
    summed = rotate(summed, z)
    summed = scatter_ring([summed[k] for k in range(4)], deep)
    q_block = summed[:HALF].astype(BF)
    scale = lax.rsqrt(summed[HALF : HALF + 2].reshape(HALF) + EPSILON)

    p_tile = after(p_tile, q_block).transpose(1, 0, 2, 3, 4).reshape(16 * rows, HALF)
    p_tile_other = swap_cores(p_tile)

    left_part, right_part = q_block[:, :64].T, q_block[:, 64:].T
    mine = jnp.where(first, left_part, right_part)
    theirs = swap_cores(jnp.where(first, right_part, left_part))
    squared = scale * scale
    left_own = (p_own * squared).astype(BF)
    left_other = swap_cores((p_other.astype(F32) * squared).astype(BF))

    q_wide = q_block.astype(F32)
    terms = three_terms(jnp.sum(q_wide * q_wide, axis=1)).reshape(6, 128)
    block = jnp.concatenate([q_block, jnp.pad(terms, ((0, 10), (0, 0))), summed[HALF + 16 :].astype(BF)], 0)
    stack = rotate(jnp.stack(gather_ring(block, deep)), (4 - z) % 4)
    unit = stack.transpose(1, 0, 2).reshape(TALL, UNIT)
    slab = jnp.stack(gather_ring(unit, middle))
    slab, mine, theirs, left_own, left_other, early = lax.optimization_barrier(
        (slab, mine, theirs, left_own, left_other, early)
    )
    q_own = gather_ring(slab, big)
    q_other = [swap_cores(q_own[k]) if k != 2 else None for k in range(4)]

    near = [(k, j) for k in (0, 1, 3) for j in (0, 1, 3)]
    across = [(2, 0), (2, 1), (2, 3), (0, 2), (1, 2), (3, 2), (2, 2)]
    (new_momentum,) = update_momentum(
        orders(near), near, momentum, gradient, left_own, left_other, q_own, q_other
    )
    q_own[2] = after(q_own[2], new_momentum)
    q_other[2] = swap_cores(q_own[2])
    squares = sum_squares(q_own).reshape(HALF)
    basis_scale = lax.rsqrt(squared * squares + EPSILON)
    factors = jnp.stack([squared * basis_scale, scale * basis_scale])
    factors_other = swap_cores(factors)

    def place_of(unit):
        dx, dy = (unit // 4 - x) % 4, ((unit % 2) * 2 + (unit // 2) % 2 - y) % 4
        return [jnp.where(first, dx, dy), jnp.where(first, dy, dx)]

    block = (row % 4) * 4 + row // 4
    place = place_of(col) + place_of(block) + place_of(block + 2) + [core]
    step_scale = STEP_SIZE * math.sqrt(total_rows * width / rank)
    factors, factors_other = factors * jnp.array([[step_scale], [1.0]], F32), factors_other * jnp.array(
        [[step_scale], [1.0]], F32
    )
    tile = [
        new_momentum,
        jnp.stack(place).astype(jnp.int32),
        jnp.stack([factors[0], factors_other[0], factors[1], factors_other[1]]),
        early,
        mine,
        theirs,
        weight,
        p_tile,
        p_tile_other,
        total_rows ** (-0.5),
    ]
    new_momentum, new_weight, logits, new_basis = update_momentum(
        orders(across), across, momentum, gradient, left_own, left_other, q_own, q_other, tile
    )
    return (new_momentum, new_basis, new_weight, logits)


def solution(mesh):
    in_specs = (
        P(("row", "col"), None),
        P(("row", "col"), None),
        P(("row", "col"), None),
        P("row", "col"),
        P("col", "row"),
    )
    out_specs = (P(("row", "col"), None), P(("row", "col"), None), P("row", "col"), P("row", "col"))
    return jax.shard_map(shards, mesh=mesh, in_specs=in_specs, out_specs=out_specs, check_vma=False)
```

profile of v0, /device:TPU:1, one launch (start us, length us, event | category | flops | bytes accessed | tf_op | source)
XLA Modules:
  0.0 224.4 jit_solution(1619412896308268542)
XLA Ops:
  9.5 3.0 %collective-permute-start.4 = (bf16[32,3696]{1,0:T(8,128)(2,1)}, bf16[32,3696]{1,0:T(8,128)(2,1)S(1)}, u32[]{:S(2)}, u32[]{:S(2)}) collective-permute-start(bf16[32,3696]{1,0:T(8,128)(2,1)} %param.11), channel_id=1, source_target_pairs={{0,8},{1,9},{2,10},{3,11},{4,12},{5,13},{6,14},{7,15},{16,24},{17,... | collective-permute-start | bytes 709640 | tf_op jit(solution)/shard_map/ppermute | solution.py:39
  13.3 3.7 %collective-permute-start.2 = (bf16[128,256]{1,0:T(8,128)(2,1)S(1)}, bf16[128,256]{1,0:T(8,128)(2,1)S(1)}, u32[]{:S(2)}, u32[]{:S(2)}) collective-permute-start(bf16[128,256]{1,0:T(8,128)(2,1)S(1)} %pad_maximum_fusion.5), channel_id=1, source_target_pairs={{0,4},{1,5},{2,6},{3,7},{4,0},{5,1},{6,2},{7,3},{16,20},{17,21},{1... | collective-permute-start | bytes 196616 | tf_op jit(solution)/shard_map/ppermute | solution.py:39
  27.7 7.2 %add_convert_fusion.refs_0_.refs_1_.refs_2_.refs_3_ = bf16[231,8192]{1,0:T(8,128)(2,1)} fusion(f32[231,8192]{1,0:T(8,128)} %m_ref.3, bf16[231,8192]{1,0:T(8,128)(2,1)} %g_ref.3), kind=kLoop, calls=%fused_computation | loop fusion | flops 5677056 | bytes 15138816 | tf_op jit(solution)/shard_map/convert_element_type | solution.py:454
  40.3 13.1 %all-gather.4.cloned.1.call-done = bf16[512,3696]{1,0:T(8,128)(2,1)} async-done(((bf16[64,3696]{1,0:T(8,128)(2,1)}), bf16[512,3696]{1,0:T(8,128)(2,1)}) %all-gather.4.cloned.1.call-update) | async-done | bytes 3784720 | tf_op jit(solution)/shard_map/all_gather | solution.py:460
  53.4 5.4 %convolution_convert_fusion = bf16[512,512]{1,0:T(8,128)(2,1)S(1)} fusion(bf16[512,3696]{1,0:T(8,128)(2,1)} %all-gather.4.cloned.1.call-done, bf16[3696,512]{1,0:T(8,128)(2,1)} %refs_14_.1), kind=kOutput, calls=%fused_computation.3 | convolution fusion | flops 1938030592 | bytes 8093696 | tf_op jit(solution)/shard_map/dot_general | solution.py:468
  62.1 5.9 %shard_map.102 = (f32[231,256]{1,0:T(8,128)S(1)}, f32[231,256]{1,0:T(8,128)S(1)}) custom-call(s32[12]{0:T(128)S(1)} %stack.245.order_ref, bf16[231,8192]{1,0:T(8,128)(2,1)} %add_convert_fusion.refs_0_.refs_1_.refs_2_.refs_3_, bf16[231,8192]{1,0:T(8,128)(2,1)} %add_convert_fusion.refs_0_.refs_1_.refs_2_.refs_3_, ...), custom_call_target="tpu_custom_call" | custom-call | tf_op jit(solution)/shard_map/pallas_call | solution.py:152
  68.0 3.1 %shard_map.103 = (f32[231,256]{1,0:T(8,128)S(1)}, bf16[231,256]{1,0:T(8,128)(2,1)S(1)}, bf16[231,256]{1,0:T(8,128)(2,1)S(1)}, bf16[16,32,512]{2,1,0:T(8,128)(2,1)S(1)}) custom-call(s32[4]{0:T(128)S(1)} %pad_add_fusion.1.order_ref, bf16[231,8192]{1,0:T(8,128)(2,1)} %add_convert_fusion.refs_0_.refs_1_.refs_2_.refs_3_, ...), custom_call_target="tpu_custom_call" | custom-call | tf_op jit(solution)/shard_map/pallas_call | solution.py:152
  71.1 2.9 %shard_map.105 = bf16[4,288,512]{2,1,0:T(8,128)(2,1)S(1)} custom-call(s32[4]{0:T(128)S(1)} %pad_add_fusion.1.order_ref, bf16[231,8192]{1,0:T(8,128)(2,1)} %add_convert_fusion.refs_0_.refs_1_.refs_2_.refs_3_, bf16[231,8192]{1,0:T(8,128)(2,1)} %add_convert_fusion.refs_0_.refs_1_.refs_2_.refs_3_, ...), custom_call_target="tpu_custom_call" | custom-call | tf_op jit(solution)/shard_map/pallas_call | solution.py:186
  75.6 5.3 %shard_map.106 = (bf16[4,288,512]{2,1,0:T(8,128)(2,1)}, bf16[4,288,512]{2,1,0:T(8,128)(2,1)}) custom-call(s32[8]{0:T(128)S(1)} %stack.255.order_ref, bf16[231,8192]{1,0:T(8,128)(2,1)} %add_convert_fusion.refs_0_.refs_1_.refs_2_.refs_3_, bf16[231,8192]{1,0:T(8,128)(2,1)} %add_convert_fusion.refs_0_.refs_1_.refs_2_.refs_3_, ...), custom_call_target="tpu_custom_call" | custom-call | tf_op jit(solution)/shard_map/pallas_call | solution.py:186
  80.9 2.7 %collective-permute-start.15 = (bf16[4,288,512]{2,1,0:T(8,128)(2,1)}, bf16[4,288,512]{2,1,0:T(8,128)(2,1)}, u32[]{:S(2)}, u32[]{:S(2)}) collective-permute-start(bf16[4,288,512]{2,1,0:T(8,128)(2,1)} %get-tuple-element.60), channel_id=1, source_target_pairs={{0,32},{1,17},{2,34},{3,19},{4,36},{5,21},{6,38},{7,23},{16,48},{1... | collective-permute-start | bytes 3538952 | tf_op jit(solution)/shard_map/ppermute | solution.py:39
  86.4 2.9 %shard_map.104 = bf16[4,288,512]{2,1,0:T(8,128)(2,1)S(1)} custom-call(s32[4]{0:T(128)S(1)} %pad_add_fusion.order_ref, bf16[231,8192]{1,0:T(8,128)(2,1)} %add_convert_fusion.refs_0_.refs_1_.refs_2_.refs_3_, bf16[231,8192]{1,0:T(8,128)(2,1)} %add_convert_fusion.refs_0_.refs_1_.refs_2_.refs_3_, ...), custom_call_target="tpu_custom_call" | custom-call | tf_op jit(solution)/shard_map/pallas_call | solution.py:186
  89.3 22.1 %collective-permute-done.14 = bf16[2,231,256]{2,1,0:T(8,128)(2,1)S(1)} collective-permute-done((bf16[2,231,256]{2,1,0:T(8,128)(2,1)S(1)}, bf16[2,231,256]{2,1,0:T(8,128)(2,1)S(1)}, u32[]{:S(2)}, u32[]{:S(2)}) %collective-permute-start.14) | collective-permute-done | bytes 236576 | tf_op jit(solution)/shard_map/ppermute | solution.py:39
  112.7 3.7 %collective-permute-done.13 = bf16[2,2,64,512]{3,2,0,1:T(8,128)(2,1)} collective-permute-done((bf16[2,2,64,512]{3,2,0,1:T(8,128)(2,1)}, bf16[2,2,64,512]{3,2,0,1:T(8,128)(2,1)}, u32[]{:S(2)}, u32[]{:S(2)}) %collective-permute-start.13) | collective-permute-done | bytes 262176 | tf_op jit(solution)/shard_map/ppermute | solution.py:53
  120.7 3.7 %collective-permute-start.17 = (bf16[288,512]{1,0:T(8,128)(2,1)S(1)}, bf16[288,512]{1,0:T(8,128)(2,1)S(1)}, u32[]{:S(2)}, u32[]{:S(2)}) collective-permute-start(bf16[288,512]{1,0:T(8,128)(2,1)S(1)} %get-tuple-element.84), channel_id=1, source_target_pairs={{0,8},{1,65},{2,10},{3,67},{4,12},{5,69},{6,14},{7,71},{16,24},{17... | collective-permute-start | bytes 884744 | tf_op jit(solution)/shard_map/ppermute | solution.py:39
  125.9 4.6 %collective-permute-done.17 = bf16[288,512]{1,0:T(8,128)(2,1)S(1)} collective-permute-done((bf16[288,512]{1,0:T(8,128)(2,1)S(1)}, bf16[288,512]{1,0:T(8,128)(2,1)S(1)}, u32[]{:S(2)}, u32[]{:S(2)}) %collective-permute-start.17) | collective-permute-done | bytes 294944 | tf_op jit(solution)/shard_map/ppermute | solution.py:39
  140.7 3.5 %collective-permute-done.21 = bf16[288,128]{0,1:T(8,128)(2,1)S(1)} collective-permute-done((bf16[288,128]{0,1:T(8,128)(2,1)S(1)}, bf16[288,128]{0,1:T(8,128)(2,1)S(1)}, u32[]{:S(2)}, u32[]{:S(2)}) %collective-permute-start.21) | collective-permute-done | bytes 73760 | tf_op jit(solution)/shard_map/ppermute | solution.py:39
  154.2 3.3 %collective-permute-start.28 = (bf16[288,512]{1,0:T(8,128)(2,1)S(1)}, bf16[288,512]{1,0:T(8,128)(2,1)S(1)}, u32[]{:S(2)}, u32[]{:S(2)}) collective-permute-start(bf16[288,512]{1,0:T(8,128)(2,1)S(1)} %copy.48), channel_id=1, source_target_pairs={{0,8},{1,65},{2,10},{3,67},{4,12},{5,69},{6,14},{7,71},{16,24},{17... | collective-permute-start | bytes 884744 | tf_op jit(solution)/shard_map/ppermute | solution.py:39
  160.9 3.8 %collective-permute-done.28 = bf16[288,512]{1,0:T(8,128)(2,1)S(1)} collective-permute-done((bf16[288,512]{1,0:T(8,128)(2,1)S(1)}, bf16[288,512]{1,0:T(8,128)(2,1)S(1)}, u32[]{:S(2)}, u32[]{:S(2)}) %collective-permute-start.28) | collective-permute-done | bytes 294944 | tf_op jit(solution)/shard_map/ppermute | solution.py:39
  166.2 2.7 %collective-permute-start.33 = (bf16[4,288,512]{2,1,0:T(8,128)(2,1)S(1)}, bf16[4,288,512]{2,1,0:T(8,128)(2,1)S(1)}, u32[]{:S(2)}, u32[]{:S(2)}) collective-permute-start(bf16[4,288,512]{2,1,0:T(8,128)(2,1)S(1)} %pad_maximum_fusion.refs_0_), channel_id=1, source_target_pairs={{0,96},{1,25},{2,98},{3,27},{4,100},{5,29},{6,102},{7,31},{16,112}... | collective-permute-start | bytes 3538952 | tf_op jit(solution)/shard_map/ppermute | solution.py:39
  168.8 13.6 %collective-permute-done.35.refs_2_.refs_3_ = bf16[4,288,512]{2,1,0:T(8,128)(2,1)S(1)} collective-permute-done((bf16[4,288,512]{2,1,0:T(8,128)(2,1)S(1)}, bf16[4,288,512]{2,1,0:T(8,128)(2,1)S(1)}, u32[]{:S(2)}, u32[]{:S(2)}) %collective-permute-start.35) | collective-permute-done | bytes 1179680 | tf_op jit(solution)/shard_map/ppermute | solution.py:39
  183.6 3.0 %copy.62 = bf16[4,2,2,231,256]{4,3,2,0,1:T(8,128)(2,1)} copy(bf16[4,2,2,231,256]{4,2,3,1,0:T(2,128)(2,1)} %bitcast.139) | data formatting | bytes 3784704 | tf_op jit(solution)/shard_map/optimization_barrier | solution.py:88
  186.6 2.7 %reshape.155.refs_15_ = bf16[3696,256]{1,0:T(8,128)(2,1)} reshape(bf16[2,4,2,231,256]{4,3,2,1,0:T(8,128)(2,1)} %bitcast.133) | data formatting | bytes 3784704 | tf_op jit(solution)/shard_map/reshape | solution.py:504
  194.5 6.6 %shard_map.107.refs_8_ = f32[231,8192]{1,0:T(8,128)} custom-call(s32[9]{0:T(128)S(1)} %stack.265.order_ref, bf16[231,256]{1,0:T(8,128)(2,1)S(1)} %copy-done, bf16[231,256]{1,0:T(8,128)(2,1)S(1)} %copy-done.3, f32[231,8192]{1,0:T(8,128)} %m_ref.3, bf16[231,8192]{1,0:T(8,128)(2,1)} %g_ref.3, bf16[4,288,512]{2,1,0:T(8,128)(2,1)S(1)} %pad_maximum_fusion.refs_0_, ...), custom_call_target="tpu_custom_call" | custom-call | tf_op jit(solution)/shard_map/pallas_call | solution.py:372
  205.4 12.1 %shard_map.109 = (f32[231,8192]{1,0:T(8,128)}, bf16[3696,512]{1,0:T(8,128)(2,1)}, bf16[64,512]{1,0:T(8,128)(2,1)}, bf16[64,512]{1,0:T(8,128)(2,1)}) custom-call(s32[7]{0:T(128)S(1)} %stack.224.order_ref, bf16[231,256]{1,0:T(8,128)(2,1)S(1)} %copy-done.1, bf16[231,256]{1,0:T(8,128)(2,1)S(1)} %copy-done.3, ...), custom_call_target="tpu_custom_call", output_to_operand_aliasing={{0}: (13, {})} | custom-call | tf_op jit(solution)/shard_map/pallas_call | solution.py:372
  (177 shorter events, 69.0 us)
Async XLA Ops:
  7.2 46.2 %all-gather.4.cloned.1.call-start = ((), (), s32[]{:S(2)}) async-start(), calls=%async_computation | async-start | bytes 4276224 | tf_op jit(solution)/shard_map/all_gather | solution.py:460
  9.5 12.3 %collective-permute-start.4 = (bf16[32,3696]{1,0:T(8,128)(2,1)}, bf16[32,3696]{1,0:T(8,128)(2,1)S(1)}, u32[]{:S(2)}, u32[]{:S(2)}) collective-permute-start(bf16[32,3696]{1,0:T(8,128)(2,1)} %param.11), channel_id=1, source_target_pairs={{0,8},{1,9},{2,10},{3,11},{4,12},{5,13},{6,14},{7,15},{16,24},{17,... | collective-permute-start | bytes 709640 | tf_op jit(solution)/shard_map/ppermute | solution.py:39
  22.8 160.9 %all-gather.6.cloned.1.call-start = ((), (), s32[]{:S(2)}) async-start(), calls=%async_computation.1 | async-start | bytes 2365440 | tf_op jit(solution)/shard_map/all_gather | solution.py:44
  22.8 12.1 %collective-permute-start.7 = (bf16[512,256]{1,0:T(8,128)(2,1)S(1)}, bf16[512,256]{1,0:T(8,128)(2,1)S(1)}, u32[]{:S(2)}, u32[]{:S(2)}) collective-permute-start(bf16[512,256]{1,0:T(8,128)(2,1)S(1)} %bitcast.141), channel_id=1, source_target_pairs={{0,16},{1,33},{2,18},{3,35},{4,20},{5,37},{6,22},{7,39},{16,8},{17... | collective-permute-start | bytes 786440 | tf_op jit(solution)/shard_map/ppermute | solution.py:39
  24.1 10.8 %collective-permute-start.6 = (bf16[512,256]{1,0:T(8,128)(2,1)S(1)}, bf16[512,256]{1,0:T(8,128)(2,1)S(1)}, u32[]{:S(2)}, u32[]{:S(2)}) collective-permute-start(bf16[512,256]{1,0:T(8,128)(2,1)S(1)} %bitcast.142), channel_id=1, source_target_pairs={{0,8},{1,65},{2,10},{3,67},{4,12},{5,69},{6,14},{7,71},{16,24},{17... | collective-permute-start | bytes 786440 | tf_op jit(solution)/shard_map/ppermute | solution.py:39
  35.1 27.0 %collective-permute-start.8 = (bf16[231,8192]{1,0:T(8,128)(2,1)}, bf16[231,8192]{1,0:T(8,128)(2,1)}, u32[]{:S(2)}, u32[]{:S(2)}) collective-permute-start(bf16[231,8192]{1,0:T(8,128)(2,1)} %add_convert_fusion.refs_0_.refs_1_.refs_2_.refs_3_), channel_id=1, source_target_pairs={{0,1},{1,0},{2,3},{3,2},{4,5},{5,4},{6,7},{7,6},{8,9},{9,8},{10,11... | collective-permute-start | bytes 11354120 | tf_op jit(solution)/shard_map/ppermute | solution.py:61
  36.4 24.0 %collective-permute-start.11 = (bf16[4,512,256]{2,1,0:T(8,128)(2,1)S(1)}, bf16[4,512,256]{2,1,0:T(8,128)(2,1)S(1)}, u32[]{:S(2)}, u32[]{:S(2)}) collective-permute-start(bf16[4,512,256]{2,1,0:T(8,128)(2,1)S(1)} %pad_maximum_fusion.1.refs_8_), channel_id=1, source_target_pairs={{0,32},{1,17},{2,34},{3,19},{4,36},{5,21},{6,38},{7,23},{16,48},{1... | collective-permute-start | bytes 3145736 | tf_op jit(solution)/shard_map/ppermute | solution.py:39
  36.6 25.5 %collective-permute-start.10 = (bf16[4,512,256]{2,1,0:T(8,128)(2,1)S(1)}, bf16[4,512,256]{2,1,0:T(8,128)(2,1)}, u32[]{:S(2)}, u32[]{:S(2)}) collective-permute-start(bf16[4,512,256]{2,1,0:T(8,128)(2,1)S(1)} %pad_maximum_fusion.1.refs_8_), channel_id=1, source_target_pairs={{0,96},{1,25},{2,98},{3,27},{4,100},{5,29},{6,102},{7,31},{16,112}... | collective-permute-start | bytes 3145736 | tf_op jit(solution)/shard_map/ppermute | solution.py:39
  39.1 28.9 %collective-permute-start.9 = (bf16[4,512,256]{2,1,0:T(8,128)(2,1)S(1)}, bf16[4,512,256]{2,1,0:T(8,128)(2,1)S(1)}, u32[]{:S(2)}, u32[]{:S(2)}) collective-permute-start(bf16[4,512,256]{2,1,0:T(8,128)(2,1)S(1)} %pad_maximum_fusion.1.refs_8_), channel_id=1, source_target_pairs={{0,64},{1,9},{2,66},{3,11},{4,68},{5,13},{6,70},{7,15},{16,80},{17... | collective-permute-start | bytes 3145736 | tf_op jit(solution)/shard_map/ppermute | solution.py:39
  74.0 43.5 %collective-permute-start.12 = (bf16[4,288,512]{2,1,0:T(8,128)(2,1)S(1)}, bf16[4,288,512]{2,1,0:T(8,128)(2,1)}, u32[]{:S(2)}, u32[]{:S(2)}) collective-permute-start(bf16[4,288,512]{2,1,0:T(8,128)(2,1)S(1)} %shard_map.105), channel_id=1, source_target_pairs={{0,64},{1,9},{2,66},{3,11},{4,68},{5,13},{6,70},{7,15},{16,80},{17... | collective-permute-start | bytes 3538952 | tf_op jit(solution)/shard_map/ppermute | solution.py:39
  80.9 36.6 %collective-permute-start.15 = (bf16[4,288,512]{2,1,0:T(8,128)(2,1)}, bf16[4,288,512]{2,1,0:T(8,128)(2,1)}, u32[]{:S(2)}, u32[]{:S(2)}) collective-permute-start(bf16[4,288,512]{2,1,0:T(8,128)(2,1)} %get-tuple-element.60), channel_id=1, source_target_pairs={{0,32},{1,17},{2,34},{3,19},{4,36},{5,21},{6,38},{7,23},{16,48},{1... | collective-permute-start | bytes 3538952 | tf_op jit(solution)/shard_map/ppermute | solution.py:39
  83.6 33.9 %collective-permute-start.16 = (bf16[4,288,512]{2,1,0:T(8,128)(2,1)}, bf16[4,288,512]{2,1,0:T(8,128)(2,1)}, u32[]{:S(2)}, u32[]{:S(2)}) collective-permute-start(bf16[4,288,512]{2,1,0:T(8,128)(2,1)} %get-tuple-element.61), channel_id=1, source_target_pairs={{0,96},{1,25},{2,98},{3,27},{4,100},{5,29},{6,102},{7,31},{16,112}... | collective-permute-start | bytes 3538952 | tf_op jit(solution)/shard_map/ppermute | solution.py:39
  83.7 27.8 %collective-permute-start.14 = (bf16[2,231,256]{2,1,0:T(8,128)(2,1)S(1)}, bf16[2,231,256]{2,1,0:T(8,128)(2,1)S(1)}, u32[]{:S(2)}, u32[]{:S(2)}) collective-permute-start(bf16[2,231,256]{2,1,0:T(8,128)(2,1)S(1)} %pad_maximum_fusion.4), channel_id=1, source_target_pairs={{0,8},{1,9},{2,10},{3,11},{4,12},{5,13},{6,14},{7,15},{16,24},{17,... | collective-permute-start | bytes 709640 | tf_op jit(solution)/shard_map/ppermute | solution.py:39
  86.4 30.0 %collective-permute-start.13 = (bf16[2,2,64,512]{3,2,0,1:T(8,128)(2,1)}, bf16[2,2,64,512]{3,2,0,1:T(8,128)(2,1)}, u32[]{:S(2)}, u32[]{:S(2)}) collective-permute-start(bf16[2,2,64,512]{3,2,0,1:T(8,128)(2,1)} %select_bitcast_fusion), channel_id=1, source_target_pairs={{0,16},{1,17},{2,18},{3,19},{4,20},{5,21},{6,22},{7,23},{16,0},{17... | collective-permute-start | bytes 786440 | tf_op jit(solution)/shard_map/ppermute | solution.py:53
  120.7 9.9 %collective-permute-start.17 = (bf16[288,512]{1,0:T(8,128)(2,1)S(1)}, bf16[288,512]{1,0:T(8,128)(2,1)S(1)}, u32[]{:S(2)}, u32[]{:S(2)}) collective-permute-start(bf16[288,512]{1,0:T(8,128)(2,1)S(1)} %get-tuple-element.84), channel_id=1, source_target_pairs={{0,8},{1,65},{2,10},{3,67},{4,12},{5,69},{6,14},{7,71},{16,24},{17... | collective-permute-start | bytes 884744 | tf_op jit(solution)/shard_map/ppermute | solution.py:39
  124.4 9.6 %collective-permute-start.19 = (bf16[288,512]{1,0:T(8,128)(2,1)S(1)}, bf16[288,512]{1,0:T(8,128)(2,1)S(1)}, u32[]{:S(2)}, u32[]{:S(2)}) collective-permute-start(bf16[288,512]{1,0:T(8,128)(2,1)S(1)} %get-tuple-element.86), channel_id=1, source_target_pairs={{0,16},{1,33},{2,18},{3,35},{4,20},{5,37},{6,22},{7,39},{16,8},{17... | collective-permute-start | bytes 884744 | tf_op jit(solution)/shard_map/ppermute | solution.py:39
  154.2 10.6 %collective-permute-start.28 = (bf16[288,512]{1,0:T(8,128)(2,1)S(1)}, bf16[288,512]{1,0:T(8,128)(2,1)S(1)}, u32[]{:S(2)}, u32[]{:S(2)}) collective-permute-start(bf16[288,512]{1,0:T(8,128)(2,1)S(1)} %copy.48), channel_id=1, source_target_pairs={{0,8},{1,65},{2,10},{3,67},{4,12},{5,69},{6,14},{7,71},{16,24},{17... | collective-permute-start | bytes 884744 | tf_op jit(solution)/shard_map/ppermute | solution.py:39
  166.2 16.3 %collective-permute-start.35 = (bf16[4,288,512]{2,1,0:T(8,128)(2,1)S(1)}, bf16[4,288,512]{2,1,0:T(8,128)(2,1)S(1)}, u32[]{:S(2)}, u32[]{:S(2)}) collective-permute-start(bf16[4,288,512]{2,1,0:T(8,128)(2,1)S(1)} %pad_maximum_fusion.refs_0_), channel_id=1, source_target_pairs={{0,32},{1,17},{2,34},{3,19},{4,36},{5,21},{6,38},{7,23},{16,48},{1... | collective-permute-start | bytes 3538952 | tf_op jit(solution)/shard_map/ppermute | solution.py:39
  166.2 16.3 %collective-permute-start.33 = (bf16[4,288,512]{2,1,0:T(8,128)(2,1)S(1)}, bf16[4,288,512]{2,1,0:T(8,128)(2,1)S(1)}, u32[]{:S(2)}, u32[]{:S(2)}) collective-permute-start(bf16[4,288,512]{2,1,0:T(8,128)(2,1)S(1)} %pad_maximum_fusion.refs_0_), channel_id=1, source_target_pairs={{0,96},{1,25},{2,98},{3,27},{4,100},{5,29},{6,102},{7,31},{16,112}... | collective-permute-start | bytes 3538952 | tf_op jit(solution)/shard_map/ppermute | solution.py:39
  168.8 23.8 %collective-permute-start.36 = (bf16[4,288,512]{2,1,0:T(8,128)(2,1)S(1)}, bf16[4,288,512]{2,1,0:T(8,128)(2,1)}, u32[]{:S(2)}, u32[]{:S(2)}) collective-permute-start(bf16[4,288,512]{2,1,0:T(8,128)(2,1)S(1)} %pad_maximum_fusion.refs_0_), channel_id=1, source_target_pairs={{0,1},{1,0},{2,3},{3,2},{4,5},{5,4},{6,7},{7,6},{8,9},{9,8},{10,11... | collective-permute-start | bytes 3538952 | tf_op jit(solution)/shard_map/ppermute | solution.py:61
  182.4 10.2 %collective-permute-start.38 = (bf16[4,288,512]{2,1,0:T(8,128)(2,1)S(1)}, bf16[4,288,512]{2,1,0:T(8,128)(2,1)}, u32[]{:S(2)}, u32[]{:S(2)}) collective-permute-start(bf16[4,288,512]{2,1,0:T(8,128)(2,1)S(1)} %collective-permute-done.35.refs_2_.refs_3_), channel_id=1, source_target_pairs={{0,1},{1,0},{2,3},{3,2},{4,5},{5,4},{6,7},{7,6},{8,9},{9,8},{10,11... | collective-permute-start | bytes 3538952 | tf_op jit(solution)/shard_map/ppermute | solution.py:61
  182.4 10.2 %collective-permute-start.37 = (bf16[4,288,512]{2,1,0:T(8,128)(2,1)S(1)}, bf16[4,288,512]{2,1,0:T(8,128)(2,1)}, u32[]{:S(2)}, u32[]{:S(2)}) collective-permute-start(bf16[4,288,512]{2,1,0:T(8,128)(2,1)S(1)} %collective-permute-done.33.refs_1_), channel_id=1, source_target_pairs={{0,1},{1,0},{2,3},{3,2},{4,5},{5,4},{6,7},{7,6},{8,9},{9,8},{10,11... | collective-permute-start | bytes 3538952 | tf_op jit(solution)/shard_map/ppermute | solution.py:61
  182.9 18.2 %collective-permute-start.34 = (bf16[4,288,512]{2,1,0:T(8,128)(2,1)S(1)}, bf16[4,288,512]{2,1,0:T(8,128)(2,1)}, u32[]{:S(2)}, u32[]{:S(2)}) collective-permute-start(bf16[4,288,512]{2,1,0:T(8,128)(2,1)S(1)} %pad_maximum_fusion.refs_0_), channel_id=1, source_target_pairs={{0,64},{1,9},{2,66},{3,11},{4,68},{5,13},{6,70},{7,15},{16,80},{17... | collective-permute-start | bytes 3538952 | tf_op jit(solution)/shard_map/ppermute | solution.py:39
  189.4 14.8 %collective-permute-start.41 = (bf16[3696,256]{1,0:T(8,128)(2,1)}, bf16[3696,256]{1,0:T(8,128)(2,1)}, u32[]{:S(2)}, u32[]{:S(2)}) collective-permute-start(bf16[3696,256]{1,0:T(8,128)(2,1)} %reshape.155.refs_15_), channel_id=1, source_target_pairs={{0,1},{1,0},{2,3},{3,2},{4,5},{5,4},{6,7},{7,6},{8,9},{9,8},{10,11... | collective-permute-start | bytes 5677064 | tf_op jit(solution)/shard_map/ppermute | solution.py:61
  (33 other events, 209.8 us)
Sparse Core Ops, SparseCore 0:
  22.9 30.4 all-gather.3
  112.8 34.3 all-gather.5
where the time goes:
time: 225 us; the launch traced here: 224 us
  waiting for transfers between devices  78.8 us (35%)
  starting transfers between devices  52.5 us (23%)
  Pallas kernels  39.7 us (18%)
  other arithmetic  18.1 us (8%)
  local copies, waits for them, and re-layouts  15.1 us (7%)
  between operations  14.6 us (6%)
  matrix products  5.41 us (2%)
    ppermute x29, waiting for transfers between devices, shift_by(): return lax.ppermute(value, ALL, pairs)  60.4 us
    ppermute x29, starting transfers between devices, shift_by(): return lax.ppermute(value, ALL, pairs)  43.7 us
    pallas_call x2, Pallas kernels, update_momentum(): pl.pallas_call(kernel, in_specs=in_specs, out_specs=out_specs, out_shape=...  18.8 us
    all_gather x1, waiting for transfers between devices, shards(): lax.all_gather(by_half(tokens, tokens_near).reshape(64, -1), 'col', axis=...  13.1 us
    pallas_call x3, Pallas kernels, project_back(): pl.pallas_call(kernel, grid_spec=pltpu.PrefetchScalarGridSpec(num_scalar_...  11.1 us
    pallas_call x2, Pallas kernels, project(): pl.pallas_call(kernel, grid_spec=pltpu.PrefetchScalarGridSpec(num_scalar_...  8.99 us
    convert_element_type x1, other arithmetic, shards(): buffer_low = (momentum_in + gradient_in.astype(F32)).astype(BF)  7.23 us
    ppermute x10, starting transfers between devices, swap_cores(): return lax.ppermute(value, ALL, [(i, i ^ 1) for i in range(128)])  6.55 us
  transfers between devices with their start and end apart: 44, of which 17 were waited for; matrix products, arithmetic and copies ran while one was open for 15% of the time, Pallas kernels for 10%

commit v1 on v0

--- a/solution.py
+++ b/solution.py
@@ -82,6 +82,10 @@
 
 def rotate(stack, start):
     return lax.dynamic_slice_in_dim(jnp.concatenate([stack, stack], 0), start, 4, 0)
+
+
+def in_hbm(value):
+    return pltpu.with_memory_space_constraint(value, pltpu.HBM)
 
 
 def after(value, *done):
@@ -204,32 +208,47 @@
 def update_momentum(order, units, momentum, gradient, left_own, left_other, q_own, q_other, tile=None):
     rows, width = momentum.shape
     count = len(units)
-    own = sorted({k for k, _ in units})
-    other = sorted({j for _, j in units})
     chunks = 3
+    parts_of = []
+    for side, slabs in enumerate((q_own, q_other)):
+        for k in sorted({unit[side] for unit in units}):
+            at = 0
+            for part in slabs[k]:
+                parts_of.append((side, k, at, part))
+                at += part.shape[0]
+
+    def find(refs, side, k, j):
+        for ref, (s, slab, at, part) in zip(refs, parts_of):
+            if s == side and slab == k and at <= j < at + part.shape[0]:
+                return ref.at[j - at, pl.ds(0, HALF)]
 
     def kernel(order_ref, lo_ref, lp_ref, m_ref, g_ref, *refs):
-        own_refs = dict(zip(own, refs))
-        other_refs = dict(zip(other, refs[len(own) :]))
-        refs = refs[len(own) + len(other) :]
+        *refs, left_all, left_sems = refs
+        slab_refs, refs = refs[: len(parts_of)], refs[len(parts_of) :]
         if tile is not None:
             _, place_ref, f_ref, *small_refs, w_ref, po_ref, pp_ref = refs[:9]
             new_ref, logits_ref, basis_ref = refs[10:13]
             (early_ref, mine_ref, theirs_ref), refs_left = refs[-4:-1], refs[:-4]
             small_sems = refs[-1]
-            w_all, po_all, pp_all, w_out, unit, scaled, lines, w_sems, unit_sems, w_out_sems = refs_left[-10:]
-            out_ref, refs = refs[9], refs_left[13:-10]
+            w_all, p_all, w_out, unit, scaled, lines, w_sems, unit_sems, w_out_sems = refs_left[-9:]
+            out_ref, refs = refs[9], refs_left[13:-9]
         else:
             out_ref, refs = refs[0], refs[1:]
-        m_all, g_all, qo_all, qp_all, out_all, in_sems, out_sems = refs
+        m_all, g_all, q_all, out_all, in_sems, out_sems = refs
+        lefts = [
+            pltpu.make_async_copy(a, left_all.at[:, pl.ds(n * HALF, HALF)], left_sems.at[n])
+            for n, a in enumerate((lo_ref, lp_ref))
+        ]
+        for copy in lefts:
+            copy.start()
         loads, stores = [], []
         for n, (k, j) in enumerate(units):
             columns = pl.ds(pl.multiple_of(order_ref[n] * UNIT, UNIT), UNIT)
             pairs = (
                 (m_ref.at[:, columns], m_all.at[n]),
                 (g_ref.at[:, columns], g_all.at[n]),
-                (own_refs[k].at[j, pl.ds(0, HALF)], qo_all.at[n]),
-                (other_refs[j].at[k, pl.ds(0, HALF)], qp_all.at[n]),
+                (find(slab_refs, 0, k, j), q_all.at[n, pl.ds(0, HALF)]),
+                (find(slab_refs, 1, j, k), q_all.at[n, pl.ds(HALF, HALF)]),
             )
             loads.append(
                 [pltpu.make_async_copy(a, b, in_sems.at[n, i]) for i, (a, b) in enumerate(pairs)]
@@ -245,29 +264,35 @@
             ]
             for copy in small:
                 copy.start()
-            wanted = []
-            for side, (slabs, far, near) in enumerate(((own_refs, 0, 1), (other_refs, 1, 0))):
-                wanted.append(
-                    [
-                        (0, pl.ds(0, HALF), unit.at[side]),
-                        (2, pl.ds(HALF + 16, 16), lines.at[side, 0]),
-                        (4, pl.ds(HALF + 16, 16), lines.at[side, 1]),
-                    ]
-                )
+            wanted = [
+                [
+                    (0, pl.ds(0, HALF), unit.at[side]),
+                    (2, pl.ds(HALF + 16, 16), lines.at[side, 0]),
+                    (4, pl.ds(HALF + 16, 16), lines.at[side, 1]),
+                ]
+                for side in range(2)
+            ]
+            for ref, (side, k, start, values) in zip(slab_refs, parts_of):
                 for n, (at, part, target) in enumerate(wanted[side]):
-                    for k in range(4):
-
-                        @pl.when(place_ref[at + far] == k)
-                        def _(slabs=slabs, side=side, n=n, at=at, near=near, part=part, target=target, k=k):
-                            source = slabs[k].at[place_ref[at + near], part]
-                            pltpu.make_async_copy(source, target, unit_sems.at[side, n]).start()
+                    near = place_ref[at + 1 - side]
+                    here = (place_ref[at + side] == k) & (near >= start)
+
+                    @pl.when(here & (near < start + values.shape[0]))
+                    def _(ref=ref, side=side, start=start, n=n, part=part, target=target, near=near):
+                        source = ref.at[near - start, part]
+                        pltpu.make_async_copy(source, target, unit_sems.at[side, n]).start()
 
             chunk = w_ref.shape[0] // chunks
             parts = [pl.ds(i * chunk, chunk) for i in range(chunks)]
+            targets = (
+                (w_ref, w_all),
+                (po_ref, p_all.at[:, pl.ds(0, HALF)]),
+                (pp_ref, p_all.at[:, pl.ds(HALF, HALF)]),
+            )
             w_loads = [
                 [
                     pltpu.make_async_copy(a.at[part], b.at[part], w_sems.at[i, n])
-                    for n, (a, b) in enumerate(((w_ref, w_all), (po_ref, po_all), (pp_ref, pp_all)))
+                    for n, (a, b) in enumerate(targets)
                 ]
                 for i, part in enumerate(parts)
             ]
@@ -278,11 +303,13 @@
             for copies in w_loads:
                 for copy in copies:
                     copy.start()
+        for copy in lefts:
+            copy.wait()
+        left = left_all[...]
         for n in range(count):
             for copy in loads[n]:
                 copy.wait()
-            change = jnp.dot(lo_ref[...], qo_all[n], preferred_element_type=F32)
-            change += jnp.dot(lp_ref[...], qp_all[n], preferred_element_type=F32)
+            change = jnp.dot(left, q_all[n], preferred_element_type=F32)
             out_all[n] = (m_all[n] + g_all[n].astype(F32)) - (1.0 - MOMENTUM_DECAY) * change
             stores[n].start()
         if tile is not None:
@@ -296,11 +323,11 @@
             late = 0.0
             for side in range(2):
                 for n, (_, part, target) in enumerate(wanted[side]):
-                    pltpu.make_async_copy(own_refs[0].at[0, part], target, unit_sems.at[side, n]).wait()
+                    pltpu.make_async_copy(slab_refs[0].at[0, part], target, unit_sems.at[side, n]).wait()
                 factor = jnp.transpose(jnp.broadcast_to(f_ref[side : side + 1], (128, HALF)))
                 for at in range(0, UNIT, 128):
                     columns = slice(at, at + 128)
-                    scaled[side, :, columns] = (
+                    scaled[side * HALF : side * HALF + HALF, columns] = (
                         unit[side, :, columns].astype(F32) * factor
                     ).astype(BF)
                 product = []
@@ -310,13 +337,12 @@
                         eight = block[:, at : at + 128]
                         product.append(jnp.concatenate([eight[:8], eight[8:]], 1))
                 product = jnp.concatenate(product, 0).astype(BF)
-                late += jnp.dot(product, scaled[side], preferred_element_type=F32)
+                late += jnp.dot(product, scaled[side * HALF : side * HALF + HALF], preferred_element_type=F32)
             logits_ref[...] = ((early_ref[...].astype(F32) - late) * tile[-1]).astype(BF)
             for i, part in enumerate(parts):
                 for copy in w_loads[i]:
                     copy.wait()
-                change = jnp.dot(po_all[part, :], scaled[0], preferred_element_type=F32)
-                change += jnp.dot(pp_all[part, :], scaled[1], preferred_element_type=F32)
+                change = jnp.dot(p_all[part, :], scaled[...], preferred_element_type=F32)
                 w_out[part, :] = (w_all[part, :].astype(F32) - change).astype(BF)
                 w_stores[i].start()
             for copy in w_stores:
@@ -327,16 +353,15 @@
     anywhere = pl.BlockSpec(memory_space=pl.ANY)
     vmem = pl.BlockSpec(memory_space=pltpu.VMEM)
     smem = pl.BlockSpec(memory_space=pltpu.SMEM)
-    operands = [order, left_own, left_other, momentum, gradient]
-    in_specs = [smem, vmem, vmem, anywhere, anywhere]
-    operands += [q_own[k] for k in own] + [q_other[j] for j in other]
-    in_specs += [anywhere] * (len(own) + len(other))
+    operands = [order, *map(in_hbm, (left_own, left_other)), momentum, gradient]
+    in_specs = [smem, anywhere, anywhere, anywhere, anywhere]
+    operands += [part for *_, part in parts_of]
+    in_specs += [anywhere] * len(parts_of)
     out_specs, out_shape = [anywhere], [jax.ShapeDtypeStruct((rows, width), F32)]
     scratch_shapes = [
         pltpu.VMEM((count, rows, UNIT), F32),
         pltpu.VMEM((count, rows, UNIT), BF),
-        pltpu.VMEM((count, HALF, UNIT), BF),
-        pltpu.VMEM((count, HALF, UNIT), BF),
+        pltpu.VMEM((count, 2 * HALF, UNIT), BF),
         pltpu.VMEM((count, rows, UNIT), F32),
         pltpu.SemaphoreType.DMA((count, 4)),
         pltpu.SemaphoreType.DMA((count,)),
@@ -344,7 +369,7 @@
     aliases = {}
     if tile is not None:
         aliases = {len(operands): 0}
-        operands += tile[:-1]
+        operands += [*tile[:3], *map(in_hbm, tile[3:6]), *tile[6:-1]]
         in_specs += [anywhere, smem, vmem] + [anywhere] * 6
         tall, tokens = tile[6].shape[0], tile[3].shape[0]
         out_specs += [anywhere, vmem, vmem]
@@ -355,11 +380,10 @@
         ]
         scratch_shapes += [
             pltpu.VMEM((tall, UNIT), BF),
-            pltpu.VMEM((tall, HALF), BF),
-            pltpu.VMEM((tall, HALF), BF),
+            pltpu.VMEM((tall, 2 * HALF), BF),
             pltpu.VMEM((tall, UNIT), BF),
             pltpu.VMEM((2, HALF, UNIT), BF),
-            pltpu.VMEM((2, HALF, UNIT), BF),
+            pltpu.VMEM((2 * HALF, UNIT), BF),
             pltpu.VMEM((2, 2, 16, UNIT), BF),
             pltpu.SemaphoreType.DMA((chunks, 3)),
             pltpu.SemaphoreType.DMA((2, 3)),
@@ -369,6 +393,7 @@
             pltpu.VMEM((tokens, HALF), BF),
             pltpu.SemaphoreType.DMA((3,)),
         ]
+    scratch_shapes += [pltpu.VMEM((rows, 2 * HALF), BF), pltpu.SemaphoreType.DMA((2,))]
     return pl.pallas_call(
         kernel,
         in_specs=in_specs,
@@ -380,20 +405,20 @@
     )(*operands)
 
 
-def sum_squares(slabs):
+def sum_squares(parts):
     def kernel(*refs):
-        total = sum(ref[u].astype(F32) for ref in refs[:4] for u in range(4))
+        total = sum(ref[u].astype(F32) for ref in refs[:-1] for u in range(ref.shape[0]))
         total = sum(total[:, at : at + 128] for at in range(0, UNIT, 128))
-        refs[4][...] = total[0:2] + total[2:4] + total[4:6]
+        refs[-1][...] = total[0:2] + total[2:4] + total[4:6]
 
     return pl.pallas_call(
         kernel,
         grid=(1,),
-        in_specs=[pl.BlockSpec((4, 16, UNIT), lambda i: (0, HALF // 16, 0))] * 4,
+        in_specs=[pl.BlockSpec((p.shape[0], 16, UNIT), lambda i: (0, HALF // 16, 0)) for p in parts],
         out_specs=pl.BlockSpec((2, 128), lambda i: (0, 0)),
         out_shape=jax.ShapeDtypeStruct((2, 128), F32),
         compiler_params=params(),
-    )(*slabs)
+    )(*parts)
 
 
 def three_terms(value):
@@ -478,31 +503,29 @@
         slab_orders(2), buffer_low, buffer_other, [pieces[2]], sums, token_parts
     )
 
+    p_chip = jnp.stack(by_core(p_own_low, p_other))
+    p_far = swap_y_hi(p_chip)
+    p_pair = by_half(p_chip, p_far)
+
     slabs = [None] * 4
     (slabs[2],) = project_back(slab_orders(2), buffer_low, buffer_other, p_own_low, p_other, below)
     slabs[1], slabs[3] = project_back(
-        slab_orders(1, 3), buffer_low, buffer_other, p_own_low, p_other, below
-    )
-    (slabs[0],) = project_back(slab_orders(0), buffer_low, buffer_other, p_own_low, p_other, below)
-    early, p_own_sent, p_other_sent, _ = lax.optimization_barrier(
-        (early, p_own_low, p_other, slabs[2])
-    )
-    early = halve((early[:, :, 0], early[:, :, 1]), row % 2, swap_y_lo)
-    p_chip = jnp.stack(by_core(p_own_sent, p_other_sent))
-    p_pair = by_half(p_chip, swap_y_hi(p_chip))
-    summed = scatter_ring(slabs, big, (early, p_pair)).astype(BF)
+        after(slab_orders(1, 3), slabs[2]), buffer_low, buffer_other, p_own_low, p_other, below
+    )
+    (slabs[0],) = project_back(after(slab_orders(0), slabs[1]), buffer_low, buffer_other, p_own_low, p_other, below)
+    summed = scatter_ring(slabs, big, (p_pair,)).astype(BF)
     p_tile = gather_z(p_pair[None])
+    early = halve((early[:, :, 0], early[:, :, 1]), row % 2, lambda v: swap_y_lo(after(v, summed)))
+    summed = scatter_ring([summed[k] for k in range(4)], middle, (early,)).astype(BF)
     early = halve((early[:, 0], early[:, 1]), x % 2, lambda v: exchange(after(v, summed), "x", 1))
-    summed = scatter_ring([summed[k] for k in range(4)], middle, (early,)).astype(BF)
-    early = halve((early[0], early[1]), x // 2, lambda v: exchange(after(v, summed), "x", 2))
     summed = summed.reshape(TALL, 4, 128).transpose(1, 0, 2)
     summed = rotate(summed, z)
-    summed = scatter_ring([summed[k] for k in range(4)], deep)
+    summed = scatter_ring([summed[k] for k in range(4)], deep, (early,))
+    early = halve((early[0], early[1]), x // 2, lambda v: exchange(after(v, summed), "x", 2))
     q_block = summed[:HALF].astype(BF)
     scale = lax.rsqrt(summed[HALF : HALF + 2].reshape(HALF) + EPSILON)
 
     p_tile = after(p_tile, q_block).transpose(1, 0, 2, 3, 4).reshape(16 * rows, HALF)
-    p_tile_other = swap_cores(p_tile)
 
     left_part, right_part = q_block[:, :64].T, q_block[:, 64:].T
     mine = jnp.where(first, left_part, right_part)
@@ -516,21 +539,25 @@
     block = jnp.concatenate([q_block, jnp.pad(terms, ((0, 10), (0, 0))), summed[HALF + 16 :].astype(BF)], 0)
     stack = rotate(jnp.stack(gather_ring(block, deep)), (4 - z) % 4)
     unit = stack.transpose(1, 0, 2).reshape(TALL, UNIT)
+    unit, mine, theirs, left_own, left_other, early = lax.optimization_barrier(
+        (unit, mine, theirs, left_own, left_other, early)
+    )
     slab = jnp.stack(gather_ring(unit, middle))
-    slab, mine, theirs, left_own, left_other, early = lax.optimization_barrier(
-        (slab, mine, theirs, left_own, left_other, early)
-    )
-    q_own = gather_ring(slab, big)
-    q_other = [swap_cores(q_own[k]) if k != 2 else None for k in range(4)]
+    q_ahead, q_before = shift_by(slab, big, -1), shift_by(slab, big, 1)
+    q_ahead, p_tile = lax.optimization_barrier((q_ahead, p_tile))
+    q_across = [shift_by(q_ahead[:2], big, -1), shift_by(q_before[2:], big, 1)]
+    p_tile_other = swap_cores(p_tile)
+    q_own = [[slab], [q_ahead], q_across, [q_before]]
+    q_other = [[swap_cores(part) for part in q_own[k]] if k != 2 else None for k in range(4)]
 
     near = [(k, j) for k in (0, 1, 3) for j in (0, 1, 3)]
     across = [(2, 0), (2, 1), (2, 3), (0, 2), (1, 2), (3, 2), (2, 2)]
     (new_momentum,) = update_momentum(
         orders(near), near, momentum, gradient, left_own, left_other, q_own, q_other
     )
-    q_own[2] = after(q_own[2], new_momentum)
-    q_other[2] = swap_cores(q_own[2])
-    squares = sum_squares(q_own).reshape(HALF)
+    *q_own[2], _ = lax.optimization_barrier((*q_own[2], new_momentum))
+    q_other[2] = [swap_cores(part) for part in q_own[2]]
+    squares = sum_squares([part for parts in q_own for part in parts]).reshape(HALF)
     basis_scale = lax.rsqrt(squared * squares + EPSILON)
     factors = jnp.stack([squared * basis_scale, scale * basis_scale])
     factors_other = swap_cores(factors)

time: 225 us -> 221 us (0.982)
  waiting for transfers between devices: 78.8 us -> 69.7 us
  starting transfers between devices: 52.5 us -> 60.6 us
    ppermute x29 -> x30, waiting for transfers between devices: 60.4 us -> 51.6 us  [shift_by(): return lax.ppermute(value, ALL, pairs)]
    ppermute x10 -> x11, starting transfers between devices: 6.55 us -> 11.4 us  [swap_cores(): return lax.ppermute(value, ALL, [(i, i ^ 1) for i in range(128)])]
    unnamed x37 -> x21, local copies, waits for them, and re-layouts: 4.28 us -> 0.81 us
    ppermute x3, starting transfers between devices: 2.25 us -> 5.2 us  [exchange(): return lax.ppermute(value, ALL, pairs)]
    ppermute x29 -> x30, starting transfers between devices: 43.7 us -> 43.9 us  [shift_by(): return lax.ppermute(value, ALL, pairs)]
  transfers between devices with their start and end apart: 44 -> 46, of which waited for: 17 -> 20; matrix products, arithmetic and copies ran while one was open for 15% -> 14% of each run, Pallas kernels for 10% -> 10%
where the time goes in v1:
time: 221 us; the launch traced here: 220 us
  waiting for transfers between devices  69.7 us (32%)
  starting transfers between devices  60.6 us (27%)
  Pallas kernels  39.3 us (18%)
  other arithmetic  16.5 us (7%)
  between operations  14.6 us (7%)
  local copies, waits for them, and re-layouts  13.8 us (6%)
  matrix products  5.41 us (2%)
    ppermute x30, waiting for transfers between devices, shift_by(): return lax.ppermute(value, ALL, pairs)  51.6 us
    ppermute x30, starting transfers between devices, shift_by(): return lax.ppermute(value, ALL, pairs)  43.9 us
    pallas_call x2, Pallas kernels, update_momentum(): pl.pallas_call(kernel, in_specs=in_specs, out_specs=out_specs, out_shape=...  18.5 us
    all_gather x1, waiting for transfers between devices, shards(): lax.all_gather(by_half(tokens, tokens_near).reshape(64, -1), 'col', axis=...  13.1 us
    ppermute x11, starting transfers between devices, swap_cores(): return lax.ppermute(value, ALL, [(i, i ^ 1) for i in range(128)])  11.4 us
    pallas_call x3, Pallas kernels, project_back(): pl.pallas_call(kernel, grid_spec=pltpu.PrefetchScalarGridSpec(num_scalar_...  11.1 us
    pallas_call x2, Pallas kernels, project(): pl.pallas_call(kernel, grid_spec=pltpu.PrefetchScalarGridSpec(num_scalar_...  8.98 us
    convert_element_type x1, other arithmetic, shards(): buffer_low = (momentum_in + gradient_in.astype(F32)).astype(BF)  7.23 us
  transfers between devices with their start and end apart: 46, of which 20 were waited for; matrix products, arithmetic and copies ran while one was open for 14% of the time, Pallas kernels for 10%

profile of v1, /device:TPU:1, one launch (start us, length us, event | category | flops | bytes accessed | tf_op | source)
XLA Modules:
  0.0 220.0 jit_solution(546314441247705530)
XLA Ops:
  9.5 3.0 %collective-permute-start.4 = (bf16[32,3696]{1,0:T(8,128)(2,1)}, bf16[32,3696]{1,0:T(8,128)(2,1)S(1)}, u32[]{:S(2)}, u32[]{:S(2)}) collective-permute-start(bf16[32,3696]{1,0:T(8,128)(2,1)} %param.11), channel_id=1, source_target_pairs={{0,8},{1,9},{2,10},{3,11},{4,12},{5,13},{6,14},{7,15},{16,24},{17,... | collective-permute-start | bytes 709640 | tf_op jit(solution)/shard_map/ppermute | solution.py:39
  13.3 3.7 %collective-permute-start.2 = (bf16[128,256]{1,0:T(8,128)(2,1)S(1)}, bf16[128,256]{1,0:T(8,128)(2,1)S(1)}, u32[]{:S(2)}, u32[]{:S(2)}) collective-permute-start(bf16[128,256]{1,0:T(8,128)(2,1)S(1)} %pad_maximum_fusion.5), channel_id=1, source_target_pairs={{0,4},{1,5},{2,6},{3,7},{4,0},{5,1},{6,2},{7,3},{16,20},{17,21},{1... | collective-permute-start | bytes 196616 | tf_op jit(solution)/shard_map/ppermute | solution.py:39
  27.7 7.2 %add_convert_fusion.refs_0_.refs_1_.refs_2_.refs_3_ = bf16[231,8192]{1,0:T(8,128)(2,1)} fusion(f32[231,8192]{1,0:T(8,128)} %m_ref.3, bf16[231,8192]{1,0:T(8,128)(2,1)} %g_ref.3), kind=kLoop, calls=%fused_computation | loop fusion | flops 5677056 | bytes 15138816 | tf_op jit(solution)/shard_map/convert_element_type | solution.py:479
  40.2 13.1 %all-gather.4.cloned.1.call-done = bf16[512,3696]{1,0:T(8,128)(2,1)} async-done(((bf16[64,3696]{1,0:T(8,128)(2,1)}), bf16[512,3696]{1,0:T(8,128)(2,1)}) %all-gather.4.cloned.1.call-update) | async-done | bytes 3784720 | tf_op jit(solution)/shard_map/all_gather | solution.py:485
  53.4 5.4 %convolution_convert_fusion = bf16[512,512]{1,0:T(8,128)(2,1)S(1)} fusion(bf16[512,3696]{1,0:T(8,128)(2,1)} %all-gather.4.cloned.1.call-done, bf16[3696,512]{1,0:T(8,128)(2,1)} %refs_16_.1), kind=kOutput, calls=%fused_computation.3 | convolution fusion | flops 1938030592 | bytes 8093696 | tf_op jit(solution)/shard_map/dot_general | solution.py:493
  62.1 5.9 %shard_map.102 = (f32[231,256]{1,0:T(8,128)S(1)}, f32[231,256]{1,0:T(8,128)S(1)}) custom-call(s32[12]{0:T(128)S(1)} %stack.249.order_ref, bf16[231,8192]{1,0:T(8,128)(2,1)} %add_convert_fusion.refs_0_.refs_1_.refs_2_.refs_3_, bf16[231,8192]{1,0:T(8,128)(2,1)} %add_convert_fusion.refs_0_.refs_1_.refs_2_.refs_3_, ...), custom_call_target="tpu_custom_call" | custom-call | tf_op jit(solution)/shard_map/pallas_call | solution.py:156
  68.0 3.1 %shard_map.103 = (f32[231,256]{1,0:T(8,128)S(1)}, bf16[231,256]{1,0:T(8,128)(2,1)S(1)}, bf16[231,256]{1,0:T(8,128)(2,1)S(1)}, bf16[16,32,512]{2,1,0:T(8,128)(2,1)S(1)}) custom-call(s32[4]{0:T(128)S(1)} %pad_add_fusion.1.order_ref, bf16[231,8192]{1,0:T(8,128)(2,1)} %add_convert_fusion.refs_0_.refs_1_.refs_2_.refs_3_, ...), custom_call_target="tpu_custom_call" | custom-call | tf_op jit(solution)/shard_map/pallas_call | solution.py:156
  71.1 2.9 %shard_map.104 = bf16[4,288,512]{2,1,0:T(8,128)(2,1)S(1)} custom-call(s32[4]{0:T(128)S(1)} %pad_add_fusion.1.order_ref, bf16[231,8192]{1,0:T(8,128)(2,1)} %add_convert_fusion.refs_0_.refs_1_.refs_2_.refs_3_, bf16[231,8192]{1,0:T(8,128)(2,1)} %add_convert_fusion.refs_0_.refs_1_.refs_2_.refs_3_, ...), custom_call_target="tpu_custom_call" | custom-call | tf_op jit(solution)/shard_map/pallas_call | solution.py:190
  75.9 5.3 %shard_map.105 = (bf16[4,288,512]{2,1,0:T(8,128)(2,1)}, bf16[4,288,512]{2,1,0:T(8,128)(2,1)}) custom-call(s32[8]{0:T(128)S(1)} %stack.238.order_ref, bf16[231,8192]{1,0:T(8,128)(2,1)} %add_convert_fusion.refs_0_.refs_1_.refs_2_.refs_3_, bf16[231,8192]{1,0:T(8,128)(2,1)} %add_convert_fusion.refs_0_.refs_1_.refs_2_.refs_3_, ...), custom_call_target="tpu_custom_call" | custom-call | tf_op jit(solution)/shard_map/pallas_call | solution.py:190
  85.6 2.9 %shard_map.106 = bf16[4,288,512]{2,1,0:T(8,128)(2,1)S(1)} custom-call(s32[4]{0:T(128)S(1)} %pad_add_fusion.order_ref, bf16[231,8192]{1,0:T(8,128)(2,1)} %add_convert_fusion.refs_0_.refs_1_.refs_2_.refs_3_, bf16[231,8192]{1,0:T(8,128)(2,1)} %add_convert_fusion.refs_0_.refs_1_.refs_2_.refs_3_, ...), custom_call_target="tpu_custom_call" | custom-call | tf_op jit(solution)/shard_map/pallas_call | solution.py:190
  88.6 20.0 %collective-permute-done.13 = bf16[2,231,256]{2,1,0:T(8,128)(2,1)S(1)} collective-permute-done((bf16[2,231,256]{2,1,0:T(8,128)(2,1)S(1)}, bf16[2,231,256]{2,1,0:T(8,128)(2,1)S(1)}, u32[]{:S(2)}, u32[]{:S(2)}) %collective-permute-start.13) | collective-permute-done | bytes 236576 | tf_op jit(solution)/shard_map/ppermute | solution.py:39
  108.7 2.6 %add_convert_fusion.1 = bf16[4,288,512]{2,1,0:T(8,128)(2,1)S(1)} fusion(bf16[4,288,512]{2,1,0:T(8,128)(2,1)} %collective-permute-done.15, bf16[4,288,512]{2,1,0:T(8,128)(2,1)} %collective-permute-done.14, bf16[4,288,512]{2,1,0:T(8,128)(2,1)} %collective-permute-done.12, bf16[4,288,512]{2,1,0:T(8,128)(2,1)S(1)} %shard_map.106), kind=kLoop, calls=%fused_computation.1 | loop fusion | flops 4718592 | bytes 5898240 | tf_op jit(solution)/shard_map/convert_element_type | solution.py:516
  113.7 2.6 %collective-permute-start.16 = (bf16[288,512]{1,0:T(8,128)(2,1)S(1)}, bf16[288,512]{1,0:T(8,128)(2,1)S(1)}, u32[]{:S(2)}, u32[]{:S(2)}) collective-permute-start(bf16[288,512]{1,0:T(8,128)(2,1)S(1)} %get-tuple-element.92), channel_id=1, source_target_pairs={{0,8},{1,65},{2,10},{3,67},{4,12},{5,69},{6,14},{7,71},{16,24},{17... | collective-permute-start | bytes 884744 | tf_op jit(solution)/shard_map/ppermute | solution.py:39
  121.1 3.4 %collective-permute-done.19 = bf16[288,512]{1,0:T(8,128)(2,1)S(1)} collective-permute-done((bf16[288,512]{1,0:T(8,128)(2,1)S(1)}, bf16[288,512]{1,0:T(8,128)(2,1)S(1)}, u32[]{:S(2)}, u32[]{:S(2)}) %collective-permute-start.19) | collective-permute-done | bytes 294944 | tf_op jit(solution)/shard_map/ppermute | solution.py:39
  129.5 4.3 %collective-permute-done.20 = bf16[288,128]{0,1:T(8,128)(2,1)S(1)} collective-permute-done((bf16[288,128]{0,1:T(8,128)(2,1)S(1)}, bf16[288,128]{0,1:T(8,128)(2,1)S(1)}, u32[]{:S(2)}, u32[]{:S(2)}) %collective-permute-start.20) | collective-permute-done | bytes 73760 | tf_op jit(solution)/shard_map/ppermute | solution.py:39
  133.8 2.8 %collective-permute-done.22 = bf16[288,128]{0,1:T(8,128)(2,1)S(1)} collective-permute-done((bf16[288,128]{0,1:T(8,128)(2,1)S(1)}, bf16[288,128]{0,1:T(8,128)(2,1)S(1)}, u32[]{:S(2)}, u32[]{:S(2)}) %collective-permute-start.22) | collective-permute-done | bytes 73760 | tf_op jit(solution)/shard_map/ppermute | solution.py:39
  144.9 3.5 %collective-permute-start.29 = (bf16[64,512]{1,0:T(8,128)(2,1)S(1)}, bf16[64,512]{1,0:T(8,128)(2,1)S(1)}, u32[]{:S(2)}, u32[]{:S(2)}) collective-permute-start(bf16[64,512]{1,0:T(8,128)(2,1)S(1)} %select_bitcast_fusion.8), channel_id=1, source_target_pairs={{0,64},{1,65},{2,66},{3,67},{4,68},{5,69},{6,70},{7,71},{16,80},{1... | collective-permute-start | bytes 196616 | tf_op jit(solution)/shard_map/ppermute | solution.py:53
  160.3 3.5 %collective-permute-done.31 = bf16[288,512]{1,0:T(8,128)(2,1)S(1)} collective-permute-done((bf16[288,512]{1,0:T(8,128)(2,1)S(1)}, bf16[288,512]{1,0:T(8,128)(2,1)S(1)}, u32[]{:S(2)}, u32[]{:S(2)}) %collective-permute-start.31) | collective-permute-done | bytes 294944 | tf_op jit(solution)/shard_map/ppermute | solution.py:39
  167.9 3.0 %copy.62 = bf16[4,2,2,231,256]{4,3,2,0,1:T(8,128)(2,1)} copy(bf16[4,2,2,231,256]{4,2,3,1,0:T(2,128)(2,1)} %bitcast.136) | data formatting | bytes 3784704 | tf_op jit(solution)/shard_map/optimization_barrier | solution.py:92
  170.9 2.8 %reshape.154.refs_17_ = bf16[3696,256]{1,0:T(8,128)(2,1)} reshape(bf16[2,4,2,231,256]{4,3,2,1,0:T(8,128)(2,1)} %bitcast.132) | data formatting | bytes 3784704 | tf_op jit(solution)/shard_map/reshape | solution.py:528
  173.7 6.0 %collective-permute-done.33.refs_1_ = bf16[4,288,512]{2,1,0:T(8,128)(2,1)S(1)} collective-permute-done((bf16[4,288,512]{2,1,0:T(8,128)(2,1)S(1)}, bf16[4,288,512]{2,1,0:T(8,128)(2,1)S(1)}, u32[]{:S(2)}, u32[]{:S(2)}) %collective-permute-start.33) | collective-permute-done | bytes 1179680 | tf_op jit(solution)/shard_map/ppermute | solution.py:39
  179.6 3.1 %collective-permute-done.35.refs_2_.refs_4_ = bf16[4,288,512]{2,1,0:T(8,128)(2,1)S(1)} collective-permute-done((bf16[4,288,512]{2,1,0:T(8,128)(2,1)S(1)}, bf16[4,288,512]{2,1,0:T(8,128)(2,1)S(1)}, u32[]{:S(2)}, u32[]{:S(2)}) %collective-permute-start.35) | collective-permute-done | bytes 1179680 | tf_op jit(solution)/shard_map/ppermute | solution.py:39
  191.1 6.7 %shard_map.107.refs_10_ = f32[231,8192]{1,0:T(8,128)} custom-call(s32[9]{0:T(128)S(1)} %stack.269.order_ref, bf16[231,256]{1,0:T(8,128)(2,1)} %get-tuple-element.71.lo_ref, bf16[231,256]{1,0:T(8,128)(2,1)} %copy-done.1, f32[231,8192]{1,0:T(8,128)} %m_ref.3, bf16[231,8192]{1,0:T(8,128)(2,1)} %g_ref.3, bf16[4,288,512]{2,1,0:T(8,128)(2,1)S(1)} %pad_maximum_fusion.refs_0_, ...), custom_call_target="tpu_custom_call" | custom-call | tf_op jit(solution)/shard_map/pallas_call | solution.py:397
  201.3 11.8 %shard_map.109 = (f32[231,8192]{1,0:T(8,128)}, bf16[3696,512]{1,0:T(8,128)(2,1)}, bf16[64,512]{1,0:T(8,128)(2,1)}, bf16[64,512]{1,0:T(8,128)(2,1)}) custom-call(s32[7]{0:T(128)S(1)} %stack.227.order_ref, bf16[231,256]{1,0:T(8,128)(2,1)} %get-tuple-element.71.lo_ref, bf16[231,256]{1,0:T(8,128)(2,1)} %copy-done.1, ...), custom_call_target="tpu_custom_call", output_to_operand_aliasing={{0}: (15, {})} | custom-call | tf_op jit(solution)/shard_map/pallas_call | solution.py:397
  (166 shorter events, 76.9 us)
Async XLA Ops:
  7.2 46.2 %all-gather.4.cloned.1.call-start = ((), (), s32[]{:S(2)}) async-start(), calls=%async_computation | async-start | bytes 4276224 | tf_op jit(solution)/shard_map/all_gather | solution.py:485
  9.5 12.3 %collective-permute-start.4 = (bf16[32,3696]{1,0:T(8,128)(2,1)}, bf16[32,3696]{1,0:T(8,128)(2,1)S(1)}, u32[]{:S(2)}, u32[]{:S(2)}) collective-permute-start(bf16[32,3696]{1,0:T(8,128)(2,1)} %param.11), channel_id=1, source_target_pairs={{0,8},{1,9},{2,10},{3,11},{4,12},{5,13},{6,14},{7,15},{16,24},{17,... | collective-permute-start | bytes 709640 | tf_op jit(solution)/shard_map/ppermute | solution.py:39
  22.8 145.1 %all-gather.6.cloned.1.call-start = ((), (), s32[]{:S(2)}) async-start(), calls=%async_computation.1 | async-start | bytes 2365440 | tf_op jit(solution)/shard_map/all_gather | solution.py:44
  22.8 12.1 %collective-permute-start.7 = (bf16[512,256]{1,0:T(8,128)(2,1)S(1)}, bf16[512,256]{1,0:T(8,128)(2,1)S(1)}, u32[]{:S(2)}, u32[]{:S(2)}) collective-permute-start(bf16[512,256]{1,0:T(8,128)(2,1)S(1)} %bitcast.140), channel_id=1, source_target_pairs={{0,16},{1,33},{2,18},{3,35},{4,20},{5,37},{6,22},{7,39},{16,8},{17... | collective-permute-start | bytes 786440 | tf_op jit(solution)/shard_map/ppermute | solution.py:39
  24.1 10.8 %collective-permute-start.6 = (bf16[512,256]{1,0:T(8,128)(2,1)S(1)}, bf16[512,256]{1,0:T(8,128)(2,1)S(1)}, u32[]{:S(2)}, u32[]{:S(2)}) collective-permute-start(bf16[512,256]{1,0:T(8,128)(2,1)S(1)} %bitcast.141), channel_id=1, source_target_pairs={{0,8},{1,65},{2,10},{3,67},{4,12},{5,69},{6,14},{7,71},{16,24},{17... | collective-permute-start | bytes 786440 | tf_op jit(solution)/shard_map/ppermute | solution.py:39
  35.1 27.0 %collective-permute-start.8 = (bf16[231,8192]{1,0:T(8,128)(2,1)}, bf16[231,8192]{1,0:T(8,128)(2,1)}, u32[]{:S(2)}, u32[]{:S(2)}) collective-permute-start(bf16[231,8192]{1,0:T(8,128)(2,1)} %add_convert_fusion.refs_0_.refs_1_.refs_2_.refs_3_), channel_id=1, source_target_pairs={{0,1},{1,0},{2,3},{3,2},{4,5},{5,4},{6,7},{7,6},{8,9},{9,8},{10,11... | collective-permute-start | bytes 11354120 | tf_op jit(solution)/shard_map/ppermute | solution.py:61
  36.4 24.5 %collective-permute-start.11 = (bf16[4,512,256]{2,1,0:T(8,128)(2,1)S(1)}, bf16[4,512,256]{2,1,0:T(8,128)(2,1)S(1)}, u32[]{:S(2)}, u32[]{:S(2)}) collective-permute-start(bf16[4,512,256]{2,1,0:T(8,128)(2,1)S(1)} %pad_maximum_fusion.1.refs_8_), channel_id=1, source_target_pairs={{0,32},{1,17},{2,34},{3,19},{4,36},{5,21},{6,38},{7,23},{16,48},{1... | collective-permute-start | bytes 3145736 | tf_op jit(solution)/shard_map/ppermute | solution.py:39
  36.6 25.5 %collective-permute-start.10 = (bf16[4,512,256]{2,1,0:T(8,128)(2,1)S(1)}, bf16[4,512,256]{2,1,0:T(8,128)(2,1)}, u32[]{:S(2)}, u32[]{:S(2)}) collective-permute-start(bf16[4,512,256]{2,1,0:T(8,128)(2,1)S(1)} %pad_maximum_fusion.1.refs_8_), channel_id=1, source_target_pairs={{0,96},{1,25},{2,98},{3,27},{4,100},{5,29},{6,102},{7,31},{16,112}... | collective-permute-start | bytes 3145736 | tf_op jit(solution)/shard_map/ppermute | solution.py:39
  39.1 28.9 %collective-permute-start.9 = (bf16[4,512,256]{2,1,0:T(8,128)(2,1)S(1)}, bf16[4,512,256]{2,1,0:T(8,128)(2,1)S(1)}, u32[]{:S(2)}, u32[]{:S(2)}) collective-permute-start(bf16[4,512,256]{2,1,0:T(8,128)(2,1)S(1)} %pad_maximum_fusion.1.refs_8_), channel_id=1, source_target_pairs={{0,64},{1,9},{2,66},{3,11},{4,68},{5,13},{6,70},{7,15},{16,80},{17... | collective-permute-start | bytes 3145736 | tf_op jit(solution)/shard_map/ppermute | solution.py:39
  74.0 34.7 %collective-permute-start.12 = (bf16[4,288,512]{2,1,0:T(8,128)(2,1)S(1)}, bf16[4,288,512]{2,1,0:T(8,128)(2,1)}, u32[]{:S(2)}, u32[]{:S(2)}) collective-permute-start(bf16[4,288,512]{2,1,0:T(8,128)(2,1)S(1)} %shard_map.104), channel_id=1, source_target_pairs={{0,64},{1,9},{2,66},{3,11},{4,68},{5,13},{6,70},{7,15},{16,80},{17... | collective-permute-start | bytes 3538952 | tf_op jit(solution)/shard_map/ppermute | solution.py:39
  81.2 27.5 %collective-permute-start.15 = (bf16[4,288,512]{2,1,0:T(8,128)(2,1)}, bf16[4,288,512]{2,1,0:T(8,128)(2,1)}, u32[]{:S(2)}, u32[]{:S(2)}) collective-permute-start(bf16[4,288,512]{2,1,0:T(8,128)(2,1)} %get-tuple-element.63), channel_id=1, source_target_pairs={{0,96},{1,25},{2,98},{3,27},{4,100},{5,29},{6,102},{7,31},{16,112}... | collective-permute-start | bytes 3538952 | tf_op jit(solution)/shard_map/ppermute | solution.py:39
  83.0 25.7 %collective-permute-start.14 = (bf16[4,288,512]{2,1,0:T(8,128)(2,1)}, bf16[4,288,512]{2,1,0:T(8,128)(2,1)}, u32[]{:S(2)}, u32[]{:S(2)}) collective-permute-start(bf16[4,288,512]{2,1,0:T(8,128)(2,1)} %get-tuple-element.60), channel_id=1, source_target_pairs={{0,32},{1,17},{2,34},{3,19},{4,36},{5,21},{6,38},{7,23},{16,48},{1... | collective-permute-start | bytes 3538952 | tf_op jit(solution)/shard_map/ppermute | solution.py:39
  83.8 24.8 %collective-permute-start.13 = (bf16[2,231,256]{2,1,0:T(8,128)(2,1)S(1)}, bf16[2,231,256]{2,1,0:T(8,128)(2,1)S(1)}, u32[]{:S(2)}, u32[]{:S(2)}) collective-permute-start(bf16[2,231,256]{2,1,0:T(8,128)(2,1)S(1)} %pad_maximum_fusion.4), channel_id=1, source_target_pairs={{0,8},{1,9},{2,10},{3,11},{4,12},{5,13},{6,14},{7,15},{16,24},{17,... | collective-permute-start | bytes 709640 | tf_op jit(solution)/shard_map/ppermute | solution.py:39
  126.7 9.8 %collective-permute-start.22 = (bf16[288,128]{0,1:T(8,128)(2,1)S(1)}, bf16[288,128]{0,1:T(8,128)(2,1)S(1)}, u32[]{:S(2)}, u32[]{:S(2)}) collective-permute-start(bf16[288,128]{0,1:T(8,128)(2,1)S(1)} %get-tuple-element.100), channel_id=1, source_target_pairs={{0,2},{1,3},{2,4},{3,5},{4,6},{5,7},{6,0},{7,1},{16,18},{17,19},{1... | collective-permute-start | bytes 221192 | tf_op jit(solution)/shard_map/ppermute | solution.py:39
  137.8 14.3 %collective-permute-start.26 = (bf16[288,128]{0,1:T(8,128)(2,1)S(1)}, bf16[288,128]{0,1:T(8,128)(2,1)S(1)}, u32[]{:S(2)}, u32[]{:S(2)}) collective-permute-start(bf16[288,128]{0,1:T(8,128)(2,1)S(1)} %get-tuple-element.87), channel_id=1, source_target_pairs={{0,2},{1,3},{2,4},{3,5},{4,6},{5,7},{6,0},{7,1},{16,18},{17,19},{1... | collective-permute-start | bytes 221192 | tf_op jit(solution)/shard_map/ppermute | solution.py:39
  138.6 13.5 %collective-permute-start.25 = (bf16[288,128]{0,1:T(8,128)(2,1)S(1)}, bf16[288,128]{0,1:T(8,128)(2,1)S(1)}, u32[]{:S(2)}, u32[]{:S(2)}) collective-permute-start(bf16[288,128]{0,1:T(8,128)(2,1)S(1)} %get-tuple-element.87), channel_id=1, source_target_pairs={{0,4},{1,5},{2,6},{3,7},{4,0},{5,1},{6,2},{7,3},{16,20},{17,21},{1... | collective-permute-start | bytes 221192 | tf_op jit(solution)/shard_map/ppermute | solution.py:39
  140.8 11.3 %collective-permute-start.24 = (bf16[288,128]{0,1:T(8,128)(2,1)S(1)}, bf16[288,128]{0,1:T(8,128)(2,1)S(1)}, u32[]{:S(2)}, u32[]{:S(2)}) collective-permute-start(bf16[288,128]{0,1:T(8,128)(2,1)S(1)} %get-tuple-element.87), channel_id=1, source_target_pairs={{0,6},{1,7},{2,0},{3,1},{4,2},{5,3},{6,4},{7,5},{16,22},{17,23},{1... | collective-permute-start | bytes 221192 | tf_op jit(solution)/shard_map/ppermute | solution.py:39
  142.3 10.0 %collective-permute-start.27 = (bf16[64,256]{1,0:T(8,128)(2,1)S(1)}, bf16[64,256]{1,0:T(8,128)(2,1)S(1)}, u32[]{:S(2)}, u32[]{:S(2)}) collective-permute-start(bf16[64,256]{1,0:T(8,128)(2,1)S(1)} %get-tuple-element.106), channel_id=1, source_target_pairs={{0,1},{1,0},{2,3},{3,2},{4,5},{5,4},{6,7},{7,6},{8,9},{9,8},{10,11... | collective-permute-start | bytes 98312 | tf_op jit(solution)/shard_map/ppermute | solution.py:61
  154.2 9.6 %collective-permute-start.31 = (bf16[288,512]{1,0:T(8,128)(2,1)S(1)}, bf16[288,512]{1,0:T(8,128)(2,1)S(1)}, u32[]{:S(2)}, u32[]{:S(2)}) collective-permute-start(bf16[288,512]{1,0:T(8,128)(2,1)S(1)} %copy.50), channel_id=1, source_target_pairs={{0,8},{1,65},{2,10},{3,67},{4,12},{5,69},{6,14},{7,71},{16,24},{17... | collective-permute-start | bytes 884744 | tf_op jit(solution)/shard_map/ppermute | solution.py:39
  164.2 15.4 %collective-permute-start.33 = (bf16[4,288,512]{2,1,0:T(8,128)(2,1)S(1)}, bf16[4,288,512]{2,1,0:T(8,128)(2,1)S(1)}, u32[]{:S(2)}, u32[]{:S(2)}) collective-permute-start(bf16[4,288,512]{2,1,0:T(8,128)(2,1)S(1)} %pad_maximum_fusion.refs_0_), channel_id=1, source_target_pairs={{0,96},{1,25},{2,98},{3,27},{4,100},{5,29},{6,102},{7,31},{16,112}... | collective-permute-start | bytes 3538952 | tf_op jit(solution)/shard_map/ppermute | solution.py:39
  166.2 16.6 %collective-permute-start.35 = (bf16[4,288,512]{2,1,0:T(8,128)(2,1)S(1)}, bf16[4,288,512]{2,1,0:T(8,128)(2,1)S(1)}, u32[]{:S(2)}, u32[]{:S(2)}) collective-permute-start(bf16[4,288,512]{2,1,0:T(8,128)(2,1)S(1)} %pad_maximum_fusion.refs_0_), channel_id=1, source_target_pairs={{0,32},{1,17},{2,34},{3,19},{4,36},{5,21},{6,38},{7,23},{16,48},{1... | collective-permute-start | bytes 3538952 | tf_op jit(solution)/shard_map/ppermute | solution.py:39
  166.2 22.8 %collective-permute-start.37 = (bf16[4,288,512]{2,1,0:T(8,128)(2,1)S(1)}, bf16[4,288,512]{2,1,0:T(8,128)(2,1)}, u32[]{:S(2)}, u32[]{:S(2)}) collective-permute-start(bf16[4,288,512]{2,1,0:T(8,128)(2,1)S(1)} %pad_maximum_fusion.refs_0_), channel_id=1, source_target_pairs={{0,1},{1,0},{2,3},{3,2},{4,5},{5,4},{6,7},{7,6},{8,9},{9,8},{10,11... | collective-permute-start | bytes 3538952 | tf_op jit(solution)/shard_map/ppermute | solution.py:61
  185.0 16.3 %collective-permute-start.43 = (bf16[3696,256]{1,0:T(8,128)(2,1)}, bf16[3696,256]{1,0:T(8,128)(2,1)}, u32[]{:S(2)}, u32[]{:S(2)}) collective-permute-start(bf16[3696,256]{1,0:T(8,128)(2,1)} %reshape.154.refs_17_), channel_id=1, source_target_pairs={{0,1},{1,0},{2,3},{3,2},{4,5},{5,4},{6,7},{7,6},{8,9},{9,8},{10,11... | collective-permute-start | bytes 5677064 | tf_op jit(solution)/shard_map/ppermute | solution.py:61
  187.2 10.6 %collective-permute-start.36 = (bf16[2,288,512]{2,1,0:T(8,128)(2,1)}, bf16[2,288,512]{2,1,0:T(8,128)(2,1)}, u32[]{:S(2)}, u32[]{:S(2)}) collective-permute-start(bf16[2,288,512]{2,1,0:T(8,128)(2,1)} %slice.131), channel_id=1, source_target_pairs={{0,32},{1,17},{2,34},{3,19},{4,36},{5,21},{6,38},{7,23},{16,48},{1... | collective-permute-start | bytes 1769480 | tf_op jit(solution)/shard_map/ppermute | solution.py:39
  (27 other events, 168.3 us)
Sparse Core Ops, SparseCore 0:
  22.9 30.4 all-gather.3
  113.7 36.8 all-gather.5

commit v2 on v1

--- a/solution.py
+++ b/solution.py
@@ -13,7 +13,7 @@
 BF = jnp.bfloat16
 F32 = jnp.float32
 ALL = ("row", "col")
-VMEM_LIMIT = 48 * 1024 * 1024
+VMEM_LIMIT = 28 * 1024 * 1024
 HALF = 256
 TALL = HALF + 32
 UNIT = 512
@@ -166,7 +166,6 @@
 def project_back(order, own, other, p_own, p_other, below):
     rows = own.shape[0]
     count = order.shape[0] // 4
-    contract = (((0,), (0,)), ((), ()))
 
     def kernel(order_ref, *refs):
         own_refs, other_refs, below_refs, outs = refs[:4], refs[4:8], refs[10:14], refs[14:]
@@ -176,13 +175,10 @@
 
             @pl.when(step == k)
             def _(out=out):
+                left_own, left_other = jnp.transpose(p_own_ref[...]), jnp.transpose(p_other_ref[...])
                 for u in range(4):
-                    value = lax.dot_general(
-                        p_own_ref[...], own_refs[u][...], contract, preferred_element_type=F32
-                    )
-                    value += lax.dot_general(
-                        p_other_ref[...], other_refs[u][...], contract, preferred_element_type=F32
-                    )
+                    value = jnp.dot(left_own, own_refs[u][...], preferred_element_type=F32)
+                    value += jnp.dot(left_other, other_refs[u][...], preferred_element_type=F32)
                     out[u, :HALF] = value.astype(BF)
                     out[u, HALF:] = below_refs[u][0]
 
@@ -353,7 +349,7 @@
     anywhere = pl.BlockSpec(memory_space=pl.ANY)
     vmem = pl.BlockSpec(memory_space=pltpu.VMEM)
     smem = pl.BlockSpec(memory_space=pltpu.SMEM)
-    operands = [order, *map(in_hbm, (left_own, left_other)), momentum, gradient]
+    operands = [order, *map(in_hbm, (left_own, left_other, momentum, gradient))]
     in_specs = [smem, anywhere, anywhere, anywhere, anywhere]
     operands += [part for *_, part in parts_of]
     in_specs += [anywhere] * len(parts_of)
@@ -369,7 +365,7 @@
     aliases = {}
     if tile is not None:
         aliases = {len(operands): 0}
-        operands += [*tile[:3], *map(in_hbm, tile[3:6]), *tile[6:-1]]
+        operands += [in_hbm(tile[0]), *tile[1:3], *map(in_hbm, tile[3:7]), *tile[7:-1]]
         in_specs += [anywhere, smem, vmem] + [anywhere] * 6
         tall, tokens = tile[6].shape[0], tile[3].shape[0]
         out_specs += [anywhere, vmem, vmem]
@@ -491,7 +487,7 @@
     ]
 
     early = jnp.dot(tokens_all, weight, preferred_element_type=F32).astype(BF)
-    early = early.reshape(4, 2, 2, 32, -1).transpose(2, 0, 1, 3, 4).reshape(2, 2, 2, 64, -1)
+    early = early.reshape(2, 2, 2, 2, 32, -1)
     pieces[3], early, *token_parts = lax.optimization_barrier((pieces[3], early, *token_parts))
 
     def halve(value, bit, send):
@@ -515,13 +511,14 @@
     (slabs[0],) = project_back(after(slab_orders(0), slabs[1]), buffer_low, buffer_other, p_own_low, p_other, below)
     summed = scatter_ring(slabs, big, (p_pair,)).astype(BF)
     p_tile = gather_z(p_pair[None])
-    early = halve((early[:, :, 0], early[:, :, 1]), row % 2, lambda v: swap_y_lo(after(v, summed)))
+    early = halve((early[:, 0], early[:, 1]), row % 2, lambda v: swap_y_lo(after(v, summed)))
     summed = scatter_ring([summed[k] for k in range(4)], middle, (early,)).astype(BF)
-    early = halve((early[:, 0], early[:, 1]), x % 2, lambda v: exchange(after(v, summed), "x", 1))
+    early = halve((early[0], early[1]), x % 2, lambda v: exchange(after(v, summed), "x", 1))
     summed = summed.reshape(TALL, 4, 128).transpose(1, 0, 2)
     summed = rotate(summed, z)
     summed = scatter_ring([summed[k] for k in range(4)], deep, (early,))
-    early = halve((early[0], early[1]), x // 2, lambda v: exchange(after(v, summed), "x", 2))
+    early = halve((early[:, 0], early[:, 1]), x // 2, lambda v: exchange(after(v, summed), "x", 2))
+    early = early.reshape(64, -1)
     q_block = summed[:HALF].astype(BF)
     scale = lax.rsqrt(summed[HALF : HALF + 2].reshape(HALF) + EPSILON)
 

time: 221 us -> 220 us (level)
  no operation moved by 1% of the time
where the time goes in v2:
time: 220 us
  waiting for transfers between devices  69.8 us (32%)
  starting transfers between devices  60.5 us (28%)
  Pallas kernels  39 us (18%)
  other arithmetic  16.5 us (8%)
  between operations  14.6 us (7%)
  local copies, waits for them, and re-layouts  13 us (6%)
  matrix products  6.22 us (3%)
    ppermute x30, waiting for transfers between devices, shift_by(): return lax.ppermute(value, ALL, pairs)  51.7 us
    ppermute x30, starting transfers between devices, shift_by(): return lax.ppermute(value, ALL, pairs)  43.8 us
    pallas_call x2, Pallas kernels, update_momentum(): pl.pallas_call(kernel, in_specs=in_specs, out_specs=out_specs, out_shape=...  18.2 us
    all_gather x1, waiting for transfers between devices, shards(): lax.all_gather(by_half(tokens, tokens_near).reshape(64, -1), 'col', axis=...  13.1 us
    ppermute x11, starting transfers between devices, swap_cores(): return lax.ppermute(value, ALL, [(i, i ^ 1) for i in range(128)])  11.4 us
    pallas_call x3, Pallas kernels, project_back(): pl.pallas_call(kernel, grid_spec=pltpu.PrefetchScalarGridSpec(num_scalar_...  11 us
    pallas_call x2, Pallas kernels, project(): pl.pallas_call(kernel, grid_spec=pltpu.PrefetchScalarGridSpec(num_scalar_...  8.98 us
    convert_element_type x1, other arithmetic, shards(): buffer_low = (momentum_in + gradient_in.astype(F32)).astype(BF)  7.23 us
  transfers between devices with their start and end apart: 46, of which 20 were waited for; matrix products, arithmetic and copies ran while one was open for 14% of the time, Pallas kernels for 10%

profile of v2, /device:TPU:1, one launch (start us, length us, event | category | flops | bytes accessed | tf_op | source)
XLA Modules:
  0.0 219.6 jit_solution(12728602934047650903)
XLA Ops:
  9.5 3.0 %collective-permute-start.4 = (bf16[32,3696]{1,0:T(8,128)(2,1)}, bf16[32,3696]{1,0:T(8,128)(2,1)S(1)}, u32[]{:S(2)}, u32[]{:S(2)}) collective-permute-start(bf16[32,3696]{1,0:T(8,128)(2,1)} %param.11), channel_id=1, source_target_pairs={{0,8},{1,9},{2,10},{3,11},{4,12},{5,13},{6,14},{7,15},{16,24},{17,... | collective-permute-start | bytes 709640 | tf_op jit(solution)/shard_map/ppermute | solution.py:39
  13.3 3.7 %collective-permute-start.2 = (bf16[128,256]{1,0:T(8,128)(2,1)S(1)}, bf16[128,256]{1,0:T(8,128)(2,1)S(1)}, u32[]{:S(2)}, u32[]{:S(2)}) collective-permute-start(bf16[128,256]{1,0:T(8,128)(2,1)S(1)} %pad_maximum_fusion.5), channel_id=1, source_target_pairs={{0,4},{1,5},{2,6},{3,7},{4,0},{5,1},{6,2},{7,3},{16,20},{17,21},{1... | collective-permute-start | bytes 196616 | tf_op jit(solution)/shard_map/ppermute | solution.py:39
  27.7 7.2 %add_convert_fusion.refs_0_.refs_1_.refs_2_.refs_3_ = bf16[231,8192]{1,0:T(8,128)(2,1)} fusion(f32[231,8192]{1,0:T(8,128)} %m_ref.3, bf16[231,8192]{1,0:T(8,128)(2,1)} %g_ref.3), kind=kLoop, calls=%fused_computation | loop fusion | flops 5677056 | bytes 15138816 | tf_op jit(solution)/shard_map/convert_element_type | solution.py:475
  40.2 13.1 %all-gather.4.cloned.1.call-done = bf16[512,3696]{1,0:T(8,128)(2,1)} async-done(((bf16[64,3696]{1,0:T(8,128)(2,1)}), bf16[512,3696]{1,0:T(8,128)(2,1)}) %all-gather.4.cloned.1.call-update) | async-done | bytes 3784720 | tf_op jit(solution)/shard_map/all_gather | solution.py:481
  54.7 6.2 %convolution_convert_fusion = bf16[512,512]{1,0:T(8,128)(2,1)} fusion(bf16[512,3696]{1,0:T(8,128)(2,1)} %all-gather.4.cloned.1.call-done, bf16[3696,512]{1,0:T(8,128)(2,1)} %refs_16_.1), kind=kOutput, calls=%fused_computation.3 | convolution fusion | flops 1938030592 | bytes 8093696 | tf_op jit(solution)/shard_map/dot_general | solution.py:489
  62.1 5.9 %shard_map.102 = (f32[231,256]{1,0:T(8,128)S(1)}, f32[231,256]{1,0:T(8,128)S(1)}) custom-call(s32[12]{0:T(128)S(1)} %stack.249.order_ref, bf16[231,8192]{1,0:T(8,128)(2,1)} %add_convert_fusion.refs_0_.refs_1_.refs_2_.refs_3_, bf16[231,8192]{1,0:T(8,128)(2,1)} %add_convert_fusion.refs_0_.refs_1_.refs_2_.refs_3_, ...), custom_call_target="tpu_custom_call" | custom-call | tf_op jit(solution)/shard_map/pallas_call | solution.py:156
  68.0 3.1 %shard_map.103 = (f32[231,256]{1,0:T(8,128)S(1)}, bf16[231,256]{1,0:T(8,128)(2,1)S(1)}, bf16[231,256]{1,0:T(8,128)(2,1)S(1)}, bf16[16,32,512]{2,1,0:T(8,128)(2,1)S(1)}) custom-call(s32[4]{0:T(128)S(1)} %pad_add_fusion.1.order_ref, bf16[231,8192]{1,0:T(8,128)(2,1)} %add_convert_fusion.refs_0_.refs_1_.refs_2_.refs_3_, ...), custom_call_target="tpu_custom_call" | custom-call | tf_op jit(solution)/shard_map/pallas_call | solution.py:156
  71.1 2.9 %shard_map.104 = bf16[4,288,512]{2,1,0:T(8,128)(2,1)S(1)} custom-call(s32[4]{0:T(128)S(1)} %pad_add_fusion.1.order_ref, bf16[231,8192]{1,0:T(8,128)(2,1)} %add_convert_fusion.refs_0_.refs_1_.refs_2_.refs_3_, bf16[231,8192]{1,0:T(8,128)(2,1)} %add_convert_fusion.refs_0_.refs_1_.refs_2_.refs_3_, ...), custom_call_target="tpu_custom_call" | custom-call | tf_op jit(solution)/shard_map/pallas_call | solution.py:186
  75.7 5.3 %shard_map.105 = (bf16[4,288,512]{2,1,0:T(8,128)(2,1)}, bf16[4,288,512]{2,1,0:T(8,128)(2,1)}) custom-call(s32[8]{0:T(128)S(1)} %stack.238.order_ref, bf16[231,8192]{1,0:T(8,128)(2,1)} %add_convert_fusion.refs_0_.refs_1_.refs_2_.refs_3_, bf16[231,8192]{1,0:T(8,128)(2,1)} %add_convert_fusion.refs_0_.refs_1_.refs_2_.refs_3_, ...), custom_call_target="tpu_custom_call" | custom-call | tf_op jit(solution)/shard_map/pallas_call | solution.py:186
  85.4 2.9 %shard_map.106 = bf16[4,288,512]{2,1,0:T(8,128)(2,1)S(1)} custom-call(s32[4]{0:T(128)S(1)} %pad_add_fusion.order_ref, bf16[231,8192]{1,0:T(8,128)(2,1)} %add_convert_fusion.refs_0_.refs_1_.refs_2_.refs_3_, bf16[231,8192]{1,0:T(8,128)(2,1)} %add_convert_fusion.refs_0_.refs_1_.refs_2_.refs_3_, ...), custom_call_target="tpu_custom_call" | custom-call | tf_op jit(solution)/shard_map/pallas_call | solution.py:186
  88.3 20.1 %collective-permute-done.13 = bf16[2,231,256]{2,1,0:T(8,128)(2,1)S(1)} collective-permute-done((bf16[2,231,256]{2,1,0:T(8,128)(2,1)S(1)}, bf16[2,231,256]{2,1,0:T(8,128)(2,1)S(1)}, u32[]{:S(2)}, u32[]{:S(2)}) %collective-permute-start.13) | collective-permute-done | bytes 236576 | tf_op jit(solution)/shard_map/ppermute | solution.py:39
  108.5 2.6 %add_convert_fusion.1 = bf16[4,288,512]{2,1,0:T(8,128)(2,1)S(1)} fusion(bf16[4,288,512]{2,1,0:T(8,128)(2,1)} %collective-permute-done.15, bf16[4,288,512]{2,1,0:T(8,128)(2,1)} %collective-permute-done.14, bf16[4,288,512]{2,1,0:T(8,128)(2,1)} %collective-permute-done.12, bf16[4,288,512]{2,1,0:T(8,128)(2,1)S(1)} %shard_map.106), kind=kLoop, calls=%fused_computation.1 | loop fusion | flops 4718592 | bytes 5898240 | tf_op jit(solution)/shard_map/convert_element_type | solution.py:512
  113.5 2.6 %collective-permute-start.16 = (bf16[288,512]{1,0:T(8,128)(2,1)S(1)}, bf16[288,512]{1,0:T(8,128)(2,1)S(1)}, u32[]{:S(2)}, u32[]{:S(2)}) collective-permute-start(bf16[288,512]{1,0:T(8,128)(2,1)S(1)} %get-tuple-element.92), channel_id=1, source_target_pairs={{0,8},{1,65},{2,10},{3,67},{4,12},{5,69},{6,14},{7,71},{16,24},{17... | collective-permute-start | bytes 884744 | tf_op jit(solution)/shard_map/ppermute | solution.py:39
  120.9 3.4 %collective-permute-done.19 = bf16[288,512]{1,0:T(8,128)(2,1)S(1)} collective-permute-done((bf16[288,512]{1,0:T(8,128)(2,1)S(1)}, bf16[288,512]{1,0:T(8,128)(2,1)S(1)}, u32[]{:S(2)}, u32[]{:S(2)}) %collective-permute-start.19) | collective-permute-done | bytes 294944 | tf_op jit(solution)/shard_map/ppermute | solution.py:39
  129.3 4.3 %collective-permute-done.20 = bf16[288,128]{0,1:T(8,128)(2,1)S(1)} collective-permute-done((bf16[288,128]{0,1:T(8,128)(2,1)S(1)}, bf16[288,128]{0,1:T(8,128)(2,1)S(1)}, u32[]{:S(2)}, u32[]{:S(2)}) %collective-permute-start.20) | collective-permute-done | bytes 73760 | tf_op jit(solution)/shard_map/ppermute | solution.py:39
  133.6 2.7 %collective-permute-done.22 = bf16[288,128]{0,1:T(8,128)(2,1)S(1)} collective-permute-done((bf16[288,128]{0,1:T(8,128)(2,1)S(1)}, bf16[288,128]{0,1:T(8,128)(2,1)S(1)}, u32[]{:S(2)}, u32[]{:S(2)}) %collective-permute-start.22) | collective-permute-done | bytes 73760 | tf_op jit(solution)/shard_map/ppermute | solution.py:39
  144.7 3.5 %collective-permute-start.29 = (bf16[2,32,512]{2,1,0:T(8,128)(2,1)S(1)}, bf16[2,32,512]{2,1,0:T(8,128)(2,1)S(1)}, u32[]{:S(2)}, u32[]{:S(2)}) collective-permute-start(bf16[2,32,512]{2,1,0:T(8,128)(2,1)S(1)} %select_bitcast_fusion.8), channel_id=1, source_target_pairs={{0,64},{1,65},{2,66},{3,67},{4,68},{5,69},{6,70},{7,71},{16,80},{1... | collective-permute-start | bytes 196616 | tf_op jit(solution)/shard_map/ppermute | solution.py:53
  160.2 3.5 %collective-permute-done.31 = bf16[288,512]{1,0:T(8,128)(2,1)S(1)} collective-permute-done((bf16[288,512]{1,0:T(8,128)(2,1)S(1)}, bf16[288,512]{1,0:T(8,128)(2,1)S(1)}, u32[]{:S(2)}, u32[]{:S(2)}) %collective-permute-start.31) | collective-permute-done | bytes 294944 | tf_op jit(solution)/shard_map/ppermute | solution.py:39
  167.7 3.0 %copy.61 = bf16[4,2,2,231,256]{4,3,2,0,1:T(8,128)(2,1)} copy(bf16[4,2,2,231,256]{4,2,3,1,0:T(2,128)(2,1)} %bitcast.134) | data formatting | bytes 3784704 | tf_op jit(solution)/shard_map/optimization_barrier | solution.py:92
  170.7 2.7 %reshape.154.refs_17_ = bf16[3696,256]{1,0:T(8,128)(2,1)} reshape(bf16[2,4,2,231,256]{4,3,2,1,0:T(8,128)(2,1)} %bitcast.130) | data formatting | bytes 3784704 | tf_op jit(solution)/shard_map/reshape | solution.py:525
  173.5 6.0 %collective-permute-done.33.refs_1_ = bf16[4,288,512]{2,1,0:T(8,128)(2,1)S(1)} collective-permute-done((bf16[4,288,512]{2,1,0:T(8,128)(2,1)S(1)}, bf16[4,288,512]{2,1,0:T(8,128)(2,1)S(1)}, u32[]{:S(2)}, u32[]{:S(2)}) %collective-permute-start.33) | collective-permute-done | bytes 1179680 | tf_op jit(solution)/shard_map/ppermute | solution.py:39
  179.5 3.1 %collective-permute-done.35.refs_2_.refs_4_ = bf16[4,288,512]{2,1,0:T(8,128)(2,1)S(1)} collective-permute-done((bf16[4,288,512]{2,1,0:T(8,128)(2,1)S(1)}, bf16[4,288,512]{2,1,0:T(8,128)(2,1)S(1)}, u32[]{:S(2)}, u32[]{:S(2)}) %collective-permute-start.35) | collective-permute-done | bytes 1179680 | tf_op jit(solution)/shard_map/ppermute | solution.py:39
  191.0 6.7 %shard_map.107.refs_10_ = f32[231,8192]{1,0:T(8,128)} custom-call(s32[9]{0:T(128)S(1)} %stack.269.order_ref, bf16[231,256]{1,0:T(8,128)(2,1)} %get-tuple-element.71.lo_ref, bf16[231,256]{1,0:T(8,128)(2,1)} %copy-done.2, f32[231,8192]{1,0:T(8,128)} %m_ref.3, bf16[231,8192]{1,0:T(8,128)(2,1)} %g_ref.3, bf16[4,288,512]{2,1,0:T(8,128)(2,1)S(1)} %pad_maximum_fusion.refs_0_, ...), custom_call_target="tpu_custom_call" | custom-call | tf_op jit(solution)/shard_map/pallas_call | solution.py:393
  201.2 11.5 %shard_map.109 = (f32[231,8192]{1,0:T(8,128)}, bf16[3696,512]{1,0:T(8,128)(2,1)}, bf16[64,512]{1,0:T(8,128)(2,1)}, bf16[64,512]{1,0:T(8,128)(2,1)}) custom-call(s32[7]{0:T(128)S(1)} %stack.227.order_ref, bf16[231,256]{1,0:T(8,128)(2,1)} %get-tuple-element.71.lo_ref, bf16[231,256]{1,0:T(8,128)(2,1)} %copy-done.2, ...), custom_call_target="tpu_custom_call", output_to_operand_aliasing={{0}: (15, {})} | custom-call | tf_op jit(solution)/shard_map/pallas_call | solution.py:393
  (167 shorter events, 75.9 us)
Async XLA Ops:
  7.2 46.2 %all-gather.4.cloned.1.call-start = ((), (), s32[]{:S(2)}) async-start(), calls=%async_computation | async-start | bytes 4276224 | tf_op jit(solution)/shard_map/all_gather | solution.py:481
  9.5 12.3 %collective-permute-start.4 = (bf16[32,3696]{1,0:T(8,128)(2,1)}, bf16[32,3696]{1,0:T(8,128)(2,1)S(1)}, u32[]{:S(2)}, u32[]{:S(2)}) collective-permute-start(bf16[32,3696]{1,0:T(8,128)(2,1)} %param.11), channel_id=1, source_target_pairs={{0,8},{1,9},{2,10},{3,11},{4,12},{5,13},{6,14},{7,15},{16,24},{17,... | collective-permute-start | bytes 709640 | tf_op jit(solution)/shard_map/ppermute | solution.py:39
  22.8 144.9 %all-gather.6.cloned.1.call-start = ((), (), s32[]{:S(2)}) async-start(), calls=%async_computation.1 | async-start | bytes 2365440 | tf_op jit(solution)/shard_map/all_gather | solution.py:44
  22.8 12.1 %collective-permute-start.7 = (bf16[512,256]{1,0:T(8,128)(2,1)S(1)}, bf16[512,256]{1,0:T(8,128)(2,1)S(1)}, u32[]{:S(2)}, u32[]{:S(2)}) collective-permute-start(bf16[512,256]{1,0:T(8,128)(2,1)S(1)} %bitcast.138), channel_id=1, source_target_pairs={{0,16},{1,33},{2,18},{3,35},{4,20},{5,37},{6,22},{7,39},{16,8},{17... | collective-permute-start | bytes 786440 | tf_op jit(solution)/shard_map/ppermute | solution.py:39
  24.1 10.8 %collective-permute-start.6 = (bf16[512,256]{1,0:T(8,128)(2,1)S(1)}, bf16[512,256]{1,0:T(8,128)(2,1)S(1)}, u32[]{:S(2)}, u32[]{:S(2)}) collective-permute-start(bf16[512,256]{1,0:T(8,128)(2,1)S(1)} %bitcast.139), channel_id=1, source_target_pairs={{0,8},{1,65},{2,10},{3,67},{4,12},{5,69},{6,14},{7,71},{16,24},{17... | collective-permute-start | bytes 786440 | tf_op jit(solution)/shard_map/ppermute | solution.py:39
  35.1 27.0 %collective-permute-start.8 = (bf16[231,8192]{1,0:T(8,128)(2,1)}, bf16[231,8192]{1,0:T(8,128)(2,1)}, u32[]{:S(2)}, u32[]{:S(2)}) collective-permute-start(bf16[231,8192]{1,0:T(8,128)(2,1)} %add_convert_fusion.refs_0_.refs_1_.refs_2_.refs_3_), channel_id=1, source_target_pairs={{0,1},{1,0},{2,3},{3,2},{4,5},{5,4},{6,7},{7,6},{8,9},{9,8},{10,11... | collective-permute-start | bytes 11354120 | tf_op jit(solution)/shard_map/ppermute | solution.py:61
  36.4 24.5 %collective-permute-start.11 = (bf16[4,512,256]{2,1,0:T(8,128)(2,1)S(1)}, bf16[4,512,256]{2,1,0:T(8,128)(2,1)S(1)}, u32[]{:S(2)}, u32[]{:S(2)}) collective-permute-start(bf16[4,512,256]{2,1,0:T(8,128)(2,1)S(1)} %pad_maximum_fusion.1.refs_8_), channel_id=1, source_target_pairs={{0,32},{1,17},{2,34},{3,19},{4,36},{5,21},{6,38},{7,23},{16,48},{1... | collective-permute-start | bytes 3145736 | tf_op jit(solution)/shard_map/ppermute | solution.py:39
  36.6 25.5 %collective-permute-start.10 = (bf16[4,512,256]{2,1,0:T(8,128)(2,1)S(1)}, bf16[4,512,256]{2,1,0:T(8,128)(2,1)}, u32[]{:S(2)}, u32[]{:S(2)}) collective-permute-start(bf16[4,512,256]{2,1,0:T(8,128)(2,1)S(1)} %pad_maximum_fusion.1.refs_8_), channel_id=1, source_target_pairs={{0,96},{1,25},{2,98},{3,27},{4,100},{5,29},{6,102},{7,31},{16,112}... | collective-permute-start | bytes 3145736 | tf_op jit(solution)/shard_map/ppermute | solution.py:39
  39.1 28.9 %collective-permute-start.9 = (bf16[4,512,256]{2,1,0:T(8,128)(2,1)S(1)}, bf16[4,512,256]{2,1,0:T(8,128)(2,1)S(1)}, u32[]{:S(2)}, u32[]{:S(2)}) collective-permute-start(bf16[4,512,256]{2,1,0:T(8,128)(2,1)S(1)} %pad_maximum_fusion.1.refs_8_), channel_id=1, source_target_pairs={{0,64},{1,9},{2,66},{3,11},{4,68},{5,13},{6,70},{7,15},{16,80},{17... | collective-permute-start | bytes 3145736 | tf_op jit(solution)/shard_map/ppermute | solution.py:39
  74.0 34.5 %collective-permute-start.12 = (bf16[4,288,512]{2,1,0:T(8,128)(2,1)S(1)}, bf16[4,288,512]{2,1,0:T(8,128)(2,1)}, u32[]{:S(2)}, u32[]{:S(2)}) collective-permute-start(bf16[4,288,512]{2,1,0:T(8,128)(2,1)S(1)} %shard_map.104), channel_id=1, source_target_pairs={{0,64},{1,9},{2,66},{3,11},{4,68},{5,13},{6,70},{7,15},{16,80},{17... | collective-permute-start | bytes 3538952 | tf_op jit(solution)/shard_map/ppermute | solution.py:39
  81.0 27.6 %collective-permute-start.15 = (bf16[4,288,512]{2,1,0:T(8,128)(2,1)}, bf16[4,288,512]{2,1,0:T(8,128)(2,1)}, u32[]{:S(2)}, u32[]{:S(2)}) collective-permute-start(bf16[4,288,512]{2,1,0:T(8,128)(2,1)} %get-tuple-element.63), channel_id=1, source_target_pairs={{0,96},{1,25},{2,98},{3,27},{4,100},{5,29},{6,102},{7,31},{16,112}... | collective-permute-start | bytes 3538952 | tf_op jit(solution)/shard_map/ppermute | solution.py:39
  82.8 25.7 %collective-permute-start.14 = (bf16[4,288,512]{2,1,0:T(8,128)(2,1)}, bf16[4,288,512]{2,1,0:T(8,128)(2,1)}, u32[]{:S(2)}, u32[]{:S(2)}) collective-permute-start(bf16[4,288,512]{2,1,0:T(8,128)(2,1)} %get-tuple-element.60), channel_id=1, source_target_pairs={{0,32},{1,17},{2,34},{3,19},{4,36},{5,21},{6,38},{7,23},{16,48},{1... | collective-permute-start | bytes 3538952 | tf_op jit(solution)/shard_map/ppermute | solution.py:39
  83.6 24.8 %collective-permute-start.13 = (bf16[2,231,256]{2,1,0:T(8,128)(2,1)S(1)}, bf16[2,231,256]{2,1,0:T(8,128)(2,1)S(1)}, u32[]{:S(2)}, u32[]{:S(2)}) collective-permute-start(bf16[2,231,256]{2,1,0:T(8,128)(2,1)S(1)} %pad_maximum_fusion.4), channel_id=1, source_target_pairs={{0,8},{1,9},{2,10},{3,11},{4,12},{5,13},{6,14},{7,15},{16,24},{17,... | collective-permute-start | bytes 709640 | tf_op jit(solution)/shard_map/ppermute | solution.py:39
  126.6 9.8 %collective-permute-start.22 = (bf16[288,128]{0,1:T(8,128)(2,1)S(1)}, bf16[288,128]{0,1:T(8,128)(2,1)S(1)}, u32[]{:S(2)}, u32[]{:S(2)}) collective-permute-start(bf16[288,128]{0,1:T(8,128)(2,1)S(1)} %get-tuple-element.100), channel_id=1, source_target_pairs={{0,2},{1,3},{2,4},{3,5},{4,6},{5,7},{6,0},{7,1},{16,18},{17,19},{1... | collective-permute-start | bytes 221192 | tf_op jit(solution)/shard_map/ppermute | solution.py:39
  137.7 14.3 %collective-permute-start.26 = (bf16[288,128]{0,1:T(8,128)(2,1)S(1)}, bf16[288,128]{0,1:T(8,128)(2,1)S(1)}, u32[]{:S(2)}, u32[]{:S(2)}) collective-permute-start(bf16[288,128]{0,1:T(8,128)(2,1)S(1)} %get-tuple-element.87), channel_id=1, source_target_pairs={{0,2},{1,3},{2,4},{3,5},{4,6},{5,7},{6,0},{7,1},{16,18},{17,19},{1... | collective-permute-start | bytes 221192 | tf_op jit(solution)/shard_map/ppermute | solution.py:39
  138.4 13.5 %collective-permute-start.25 = (bf16[288,128]{0,1:T(8,128)(2,1)S(1)}, bf16[288,128]{0,1:T(8,128)(2,1)S(1)}, u32[]{:S(2)}, u32[]{:S(2)}) collective-permute-start(bf16[288,128]{0,1:T(8,128)(2,1)S(1)} %get-tuple-element.87), channel_id=1, source_target_pairs={{0,4},{1,5},{2,6},{3,7},{4,0},{5,1},{6,2},{7,3},{16,20},{17,21},{1... | collective-permute-start | bytes 221192 | tf_op jit(solution)/shard_map/ppermute | solution.py:39
  140.6 11.3 %collective-permute-start.24 = (bf16[288,128]{0,1:T(8,128)(2,1)S(1)}, bf16[288,128]{0,1:T(8,128)(2,1)S(1)}, u32[]{:S(2)}, u32[]{:S(2)}) collective-permute-start(bf16[288,128]{0,1:T(8,128)(2,1)S(1)} %get-tuple-element.87), channel_id=1, source_target_pairs={{0,6},{1,7},{2,0},{3,1},{4,2},{5,3},{6,4},{7,5},{16,22},{17,23},{1... | collective-permute-start | bytes 221192 | tf_op jit(solution)/shard_map/ppermute | solution.py:39
  142.1 10.0 %collective-permute-start.27 = (bf16[64,256]{1,0:T(8,128)(2,1)S(1)}, bf16[64,256]{1,0:T(8,128)(2,1)S(1)}, u32[]{:S(2)}, u32[]{:S(2)}) collective-permute-start(bf16[64,256]{1,0:T(8,128)(2,1)S(1)} %get-tuple-element.106), channel_id=1, source_target_pairs={{0,1},{1,0},{2,3},{3,2},{4,5},{5,4},{6,7},{7,6},{8,9},{9,8},{10,11... | collective-permute-start | bytes 98312 | tf_op jit(solution)/shard_map/ppermute | solution.py:61
  154.0 9.6 %collective-permute-start.31 = (bf16[288,512]{1,0:T(8,128)(2,1)S(1)}, bf16[288,512]{1,0:T(8,128)(2,1)S(1)}, u32[]{:S(2)}, u32[]{:S(2)}) collective-permute-start(bf16[288,512]{1,0:T(8,128)(2,1)S(1)} %copy.49), channel_id=1, source_target_pairs={{0,8},{1,65},{2,10},{3,67},{4,12},{5,69},{6,14},{7,71},{16,24},{17... | collective-permute-start | bytes 884744 | tf_op jit(solution)/shard_map/ppermute | solution.py:39
  164.1 15.4 %collective-permute-start.33 = (bf16[4,288,512]{2,1,0:T(8,128)(2,1)S(1)}, bf16[4,288,512]{2,1,0:T(8,128)(2,1)S(1)}, u32[]{:S(2)}, u32[]{:S(2)}) collective-permute-start(bf16[4,288,512]{2,1,0:T(8,128)(2,1)S(1)} %pad_maximum_fusion.refs_0_), channel_id=1, source_target_pairs={{0,96},{1,25},{2,98},{3,27},{4,100},{5,29},{6,102},{7,31},{16,112}... | collective-permute-start | bytes 3538952 | tf_op jit(solution)/shard_map/ppermute | solution.py:39
  166.0 16.6 %collective-permute-start.35 = (bf16[4,288,512]{2,1,0:T(8,128)(2,1)S(1)}, bf16[4,288,512]{2,1,0:T(8,128)(2,1)S(1)}, u32[]{:S(2)}, u32[]{:S(2)}) collective-permute-start(bf16[4,288,512]{2,1,0:T(8,128)(2,1)S(1)} %pad_maximum_fusion.refs_0_), channel_id=1, source_target_pairs={{0,32},{1,17},{2,34},{3,19},{4,36},{5,21},{6,38},{7,23},{16,48},{1... | collective-permute-start | bytes 3538952 | tf_op jit(solution)/shard_map/ppermute | solution.py:39
  166.0 22.8 %collective-permute-start.37 = (bf16[4,288,512]{2,1,0:T(8,128)(2,1)S(1)}, bf16[4,288,512]{2,1,0:T(8,128)(2,1)}, u32[]{:S(2)}, u32[]{:S(2)}) collective-permute-start(bf16[4,288,512]{2,1,0:T(8,128)(2,1)S(1)} %pad_maximum_fusion.refs_0_), channel_id=1, source_target_pairs={{0,1},{1,0},{2,3},{3,2},{4,5},{5,4},{6,7},{7,6},{8,9},{9,8},{10,11... | collective-permute-start | bytes 3538952 | tf_op jit(solution)/shard_map/ppermute | solution.py:61
  184.9 16.3 %collective-permute-start.43 = (bf16[3696,256]{1,0:T(8,128)(2,1)}, bf16[3696,256]{1,0:T(8,128)(2,1)}, u32[]{:S(2)}, u32[]{:S(2)}) collective-permute-start(bf16[3696,256]{1,0:T(8,128)(2,1)} %reshape.154.refs_17_), channel_id=1, source_target_pairs={{0,1},{1,0},{2,3},{3,2},{4,5},{5,4},{6,7},{7,6},{8,9},{9,8},{10,11... | collective-permute-start | bytes 5677064 | tf_op jit(solution)/shard_map/ppermute | solution.py:61
  187.1 10.6 %collective-permute-start.36 = (bf16[2,288,512]{2,1,0:T(8,128)(2,1)}, bf16[2,288,512]{2,1,0:T(8,128)(2,1)}, u32[]{:S(2)}, u32[]{:S(2)}) collective-permute-start(bf16[2,288,512]{2,1,0:T(8,128)(2,1)} %slice.131), channel_id=1, source_target_pairs={{0,32},{1,17},{2,34},{3,19},{4,36},{5,21},{6,38},{7,23},{16,48},{1... | collective-permute-start | bytes 1769480 | tf_op jit(solution)/shard_map/ppermute | solution.py:39
  (28 other events, 171.8 us)
Sparse Core Ops, SparseCore 0:
  22.9 30.4 all-gather.3
  113.5 36.8 all-gather.5

commit v3 on v2

--- a/solution.py
+++ b/solution.py
@@ -536,12 +536,12 @@
     block = jnp.concatenate([q_block, jnp.pad(terms, ((0, 10), (0, 0))), summed[HALF + 16 :].astype(BF)], 0)
     stack = rotate(jnp.stack(gather_ring(block, deep)), (4 - z) % 4)
     unit = stack.transpose(1, 0, 2).reshape(TALL, UNIT)
-    unit, mine, theirs, left_own, left_other, early = lax.optimization_barrier(
-        (unit, mine, theirs, left_own, left_other, early)
+    unit, left_own, left_other, early = lax.optimization_barrier(
+        (unit, left_own, left_other, early)
     )
     slab = jnp.stack(gather_ring(unit, middle))
     q_ahead, q_before = shift_by(slab, big, -1), shift_by(slab, big, 1)
-    q_ahead, p_tile = lax.optimization_barrier((q_ahead, p_tile))
+    q_ahead, p_tile, mine, theirs = lax.optimization_barrier((q_ahead, p_tile, mine, theirs))
     q_across = [shift_by(q_ahead[:2], big, -1), shift_by(q_before[2:], big, 1)]
     p_tile_other = swap_cores(p_tile)
     q_own = [[slab], [q_ahead], q_across, [q_before]]

time: 220 us -> 220 us (level)
  waiting for transfers between devices: 69.8 us -> 66.9 us
  starting transfers between devices: 60.5 us -> 62.8 us
    ppermute x11, starting transfers between devices: 11.4 us -> 14.4 us  [swap_cores(): return lax.ppermute(value, ALL, [(i, i ^ 1) for i in range(128)])]
  transfers between devices with their start and end apart: 46 -> 46, of which waited for: 20 -> 19; matrix products, arithmetic and copies ran while one was open for 14% -> 14% of each run, Pallas kernels for 10% -> 10%
where the time goes in v3:
time: 220 us; the launch traced here: 219 us
  waiting for transfers between devices  66.9 us (30%)
  starting transfers between devices  62.8 us (29%)
  Pallas kernels  39 us (18%)
  other arithmetic  16.5 us (8%)
  between operations  14.6 us (7%)
  local copies, waits for them, and re-layouts  13 us (6%)
  matrix products  6.22 us (3%)
    ppermute x30, waiting for transfers between devices, shift_by(): return lax.ppermute(value, ALL, pairs)  50.6 us
    ppermute x30, starting transfers between devices, shift_by(): return lax.ppermute(value, ALL, pairs)  43.7 us
    pallas_call x2, Pallas kernels, update_momentum(): pl.pallas_call(kernel, in_specs=in_specs, out_specs=out_specs, out_shape=...  18.2 us
    ppermute x11, starting transfers between devices, swap_cores(): return lax.ppermute(value, ALL, [(i, i ^ 1) for i in range(128)])  14.4 us
    all_gather x1, waiting for transfers between devices, shards(): lax.all_gather(by_half(tokens, tokens_near).reshape(64, -1), 'col', axis=...  13.1 us
    pallas_call x3, Pallas kernels, project_back(): pl.pallas_call(kernel, grid_spec=pltpu.PrefetchScalarGridSpec(num_scalar_...  11 us
    pallas_call x2, Pallas kernels, project(): pl.pallas_call(kernel, grid_spec=pltpu.PrefetchScalarGridSpec(num_scalar_...  8.98 us
    convert_element_type x1, other arithmetic, shards(): buffer_low = (momentum_in + gradient_in.astype(F32)).astype(BF)  7.23 us
  transfers between devices with their start and end apart: 46, of which 19 were waited for; matrix products, arithmetic and copies ran while one was open for 14% of the time, Pallas kernels for 10%

profile of v3, /device:TPU:1, one launch (start us, length us, event | category | flops | bytes accessed | tf_op | source)
XLA Modules:
  0.0 219.0 jit_solution(1523539224616827774)
XLA Ops:
  9.5 3.0 %collective-permute-start.4 = (bf16[32,3696]{1,0:T(8,128)(2,1)}, bf16[32,3696]{1,0:T(8,128)(2,1)S(1)}, u32[]{:S(2)}, u32[]{:S(2)}) collective-permute-start(bf16[32,3696]{1,0:T(8,128)(2,1)} %param.11), channel_id=1, source_target_pairs={{0,8},{1,9},{2,10},{3,11},{4,12},{5,13},{6,14},{7,15},{16,24},{17,... | collective-permute-start | bytes 709640 | tf_op jit(solution)/shard_map/ppermute | solution.py:39
  13.3 3.7 %collective-permute-start.2 = (bf16[128,256]{1,0:T(8,128)(2,1)S(1)}, bf16[128,256]{1,0:T(8,128)(2,1)S(1)}, u32[]{:S(2)}, u32[]{:S(2)}) collective-permute-start(bf16[128,256]{1,0:T(8,128)(2,1)S(1)} %pad_maximum_fusion.5), channel_id=1, source_target_pairs={{0,4},{1,5},{2,6},{3,7},{4,0},{5,1},{6,2},{7,3},{16,20},{17,21},{1... | collective-permute-start | bytes 196616 | tf_op jit(solution)/shard_map/ppermute | solution.py:39
  27.7 7.2 %add_convert_fusion.refs_0_.refs_1_.refs_2_.refs_3_ = bf16[231,8192]{1,0:T(8,128)(2,1)} fusion(f32[231,8192]{1,0:T(8,128)} %m_ref.3, bf16[231,8192]{1,0:T(8,128)(2,1)} %g_ref.3), kind=kLoop, calls=%fused_computation | loop fusion | flops 5677056 | bytes 15138816 | tf_op jit(solution)/shard_map/convert_element_type | solution.py:475
  40.2 13.1 %all-gather.4.cloned.1.call-done = bf16[512,3696]{1,0:T(8,128)(2,1)} async-done(((bf16[64,3696]{1,0:T(8,128)(2,1)}), bf16[512,3696]{1,0:T(8,128)(2,1)}) %all-gather.4.cloned.1.call-update) | async-done | bytes 3784720 | tf_op jit(solution)/shard_map/all_gather | solution.py:481
  54.8 6.2 %convolution_convert_fusion = bf16[512,512]{1,0:T(8,128)(2,1)} fusion(bf16[512,3696]{1,0:T(8,128)(2,1)} %all-gather.4.cloned.1.call-done, bf16[3696,512]{1,0:T(8,128)(2,1)} %refs_16_.1), kind=kOutput, calls=%fused_computation.3 | convolution fusion | flops 1938030592 | bytes 8093696 | tf_op jit(solution)/shard_map/dot_general | solution.py:489
  62.1 5.9 %shard_map.102 = (f32[231,256]{1,0:T(8,128)S(1)}, f32[231,256]{1,0:T(8,128)S(1)}) custom-call(s32[12]{0:T(128)S(1)} %stack.249.order_ref, bf16[231,8192]{1,0:T(8,128)(2,1)} %add_convert_fusion.refs_0_.refs_1_.refs_2_.refs_3_, bf16[231,8192]{1,0:T(8,128)(2,1)} %add_convert_fusion.refs_0_.refs_1_.refs_2_.refs_3_, ...), custom_call_target="tpu_custom_call" | custom-call | tf_op jit(solution)/shard_map/pallas_call | solution.py:156
  68.0 3.1 %shard_map.103 = (f32[231,256]{1,0:T(8,128)S(1)}, bf16[231,256]{1,0:T(8,128)(2,1)S(1)}, bf16[231,256]{1,0:T(8,128)(2,1)S(1)}, bf16[16,32,512]{2,1,0:T(8,128)(2,1)S(1)}) custom-call(s32[4]{0:T(128)S(1)} %pad_add_fusion.1.order_ref, bf16[231,8192]{1,0:T(8,128)(2,1)} %add_convert_fusion.refs_0_.refs_1_.refs_2_.refs_3_, ...), custom_call_target="tpu_custom_call" | custom-call | tf_op jit(solution)/shard_map/pallas_call | solution.py:156
  71.1 2.9 %shard_map.104 = bf16[4,288,512]{2,1,0:T(8,128)(2,1)S(1)} custom-call(s32[4]{0:T(128)S(1)} %pad_add_fusion.1.order_ref, bf16[231,8192]{1,0:T(8,128)(2,1)} %add_convert_fusion.refs_0_.refs_1_.refs_2_.refs_3_, bf16[231,8192]{1,0:T(8,128)(2,1)} %add_convert_fusion.refs_0_.refs_1_.refs_2_.refs_3_, ...), custom_call_target="tpu_custom_call" | custom-call | tf_op jit(solution)/shard_map/pallas_call | solution.py:186
  75.7 5.3 %shard_map.105 = (bf16[4,288,512]{2,1,0:T(8,128)(2,1)}, bf16[4,288,512]{2,1,0:T(8,128)(2,1)}) custom-call(s32[8]{0:T(128)S(1)} %stack.238.order_ref, bf16[231,8192]{1,0:T(8,128)(2,1)} %add_convert_fusion.refs_0_.refs_1_.refs_2_.refs_3_, bf16[231,8192]{1,0:T(8,128)(2,1)} %add_convert_fusion.refs_0_.refs_1_.refs_2_.refs_3_, ...), custom_call_target="tpu_custom_call" | custom-call | tf_op jit(solution)/shard_map/pallas_call | solution.py:186
  85.4 2.9 %shard_map.106 = bf16[4,288,512]{2,1,0:T(8,128)(2,1)S(1)} custom-call(s32[4]{0:T(128)S(1)} %pad_add_fusion.order_ref, bf16[231,8192]{1,0:T(8,128)(2,1)} %add_convert_fusion.refs_0_.refs_1_.refs_2_.refs_3_, bf16[231,8192]{1,0:T(8,128)(2,1)} %add_convert_fusion.refs_0_.refs_1_.refs_2_.refs_3_, ...), custom_call_target="tpu_custom_call" | custom-call | tf_op jit(solution)/shard_map/pallas_call | solution.py:186
  88.3 20.1 %collective-permute-done.13 = bf16[2,231,256]{2,1,0:T(8,128)(2,1)S(1)} collective-permute-done((bf16[2,231,256]{2,1,0:T(8,128)(2,1)S(1)}, bf16[2,231,256]{2,1,0:T(8,128)(2,1)S(1)}, u32[]{:S(2)}, u32[]{:S(2)}) %collective-permute-start.13) | collective-permute-done | bytes 236576 | tf_op jit(solution)/shard_map/ppermute | solution.py:39
  120.9 3.4 %collective-permute-done.19 = bf16[288,512]{1,0:T(8,128)(2,1)S(1)} collective-permute-done((bf16[288,512]{1,0:T(8,128)(2,1)S(1)}, bf16[288,512]{1,0:T(8,128)(2,1)S(1)}, u32[]{:S(2)}, u32[]{:S(2)}) %collective-permute-start.19) | collective-permute-done | bytes 294944 | tf_op jit(solution)/shard_map/ppermute | solution.py:39
  129.3 4.3 %collective-permute-done.20 = bf16[288,128]{0,1:T(8,128)(2,1)S(1)} collective-permute-done((bf16[288,128]{0,1:T(8,128)(2,1)S(1)}, bf16[288,128]{0,1:T(8,128)(2,1)S(1)}, u32[]{:S(2)}, u32[]{:S(2)}) %collective-permute-start.20) | collective-permute-done | bytes 73760 | tf_op jit(solution)/shard_map/ppermute | solution.py:39
  141.5 2.8 %collective-permute-start.28 = (bf16[2,32,512]{2,1,0:T(8,128)(2,1)S(1)}, bf16[2,32,512]{2,1,0:T(8,128)(2,1)S(1)}, u32[]{:S(2)}, u32[]{:S(2)}) collective-permute-start(bf16[2,32,512]{2,1,0:T(8,128)(2,1)S(1)} %select_bitcast_fusion.8), channel_id=1, source_target_pairs={{0,64},{1,65},{2,66},{3,67},{4,68},{5,69},{6,70},{7,71},{16,80},{1... | collective-permute-start | bytes 196616 | tf_op jit(solution)/shard_map/ppermute | solution.py:53
  145.1 3.5 %collective-permute-start.27 = (bf16[231,256]{1,0:T(8,128)(2,1)S(1)}, bf16[231,256]{1,0:T(8,128)(2,1)S(1)}, u32[]{:S(2)}, u32[]{:S(2)}) collective-permute-start(bf16[231,256]{1,0:T(8,128)(2,1)S(1)} %get-tuple-element.118), channel_id=1, source_target_pairs={{0,1},{1,0},{2,3},{3,2},{4,5},{5,4},{6,7},{7,6},{8,9},{9,8},{10,11... | collective-permute-start | bytes 354824 | tf_op jit(solution)/shard_map/ppermute | solution.py:61
  154.8 2.8 %collective-permute-done.31 = bf16[288,512]{1,0:T(8,128)(2,1)S(1)} collective-permute-done((bf16[288,512]{1,0:T(8,128)(2,1)S(1)}, bf16[288,512]{1,0:T(8,128)(2,1)S(1)}, u32[]{:S(2)}, u32[]{:S(2)}) %collective-permute-start.31) | collective-permute-done | bytes 294944 | tf_op jit(solution)/shard_map/ppermute | solution.py:39
  157.6 2.9 %collective-permute-done.30 = bf16[288,512]{1,0:T(8,128)(2,1)S(1)} collective-permute-done((bf16[288,512]{1,0:T(8,128)(2,1)S(1)}, bf16[288,512]{1,0:T(8,128)(2,1)S(1)}, u32[]{:S(2)}, u32[]{:S(2)}) %collective-permute-start.30) | collective-permute-done | bytes 294944 | tf_op jit(solution)/shard_map/ppermute | solution.py:39
  164.0 2.9 %collective-permute-start.37 = (bf16[4,288,512]{2,1,0:T(8,128)(2,1)S(1)}, bf16[4,288,512]{2,1,0:T(8,128)(2,1)}, u32[]{:S(2)}, u32[]{:S(2)}) collective-permute-start(bf16[4,288,512]{2,1,0:T(8,128)(2,1)S(1)} %pad_maximum_fusion.refs_0_), channel_id=1, source_target_pairs={{0,1},{1,0},{2,3},{3,2},{4,5},{5,4},{6,7},{7,6},{8,9},{9,8},{10,11... | collective-permute-start | bytes 3538952 | tf_op jit(solution)/shard_map/ppermute | solution.py:61
  167.6 3.0 %copy.61 = bf16[4,2,2,231,256]{4,3,2,0,1:T(8,128)(2,1)} copy(bf16[4,2,2,231,256]{4,2,3,1,0:T(2,128)(2,1)} %bitcast.134) | data formatting | bytes 3784704 | tf_op jit(solution)/shard_map/optimization_barrier | solution.py:92
  173.4 3.8 %collective-permute-done.32.refs_1_ = bf16[4,288,512]{2,1,0:T(8,128)(2,1)S(1)} collective-permute-done((bf16[4,288,512]{2,1,0:T(8,128)(2,1)S(1)}, bf16[4,288,512]{2,1,0:T(8,128)(2,1)S(1)}, u32[]{:S(2)}, u32[]{:S(2)}) %collective-permute-start.32) | collective-permute-done | bytes 1179680 | tf_op jit(solution)/shard_map/ppermute | solution.py:39
  177.2 3.4 %collective-permute-done.35.refs_2_.refs_4_ = bf16[4,288,512]{2,1,0:T(8,128)(2,1)S(1)} collective-permute-done((bf16[4,288,512]{2,1,0:T(8,128)(2,1)S(1)}, bf16[4,288,512]{2,1,0:T(8,128)(2,1)S(1)}, u32[]{:S(2)}, u32[]{:S(2)}) %collective-permute-start.35) | collective-permute-done | bytes 1179680 | tf_op jit(solution)/shard_map/ppermute | solution.py:39
  180.6 3.8 %collective-permute-start.39 = (bf16[4,288,512]{2,1,0:T(8,128)(2,1)S(1)}, bf16[4,288,512]{2,1,0:T(8,128)(2,1)}, u32[]{:S(2)}, u32[]{:S(2)}) collective-permute-start(bf16[4,288,512]{2,1,0:T(8,128)(2,1)S(1)} %collective-permute-done.35.refs_2_.refs_4_), channel_id=1, source_target_pairs={{0,1},{1,0},{2,3},{3,2},{4,5},{5,4},{6,7},{7,6},{8,9},{9,8},{10,11... | collective-permute-start | bytes 3538952 | tf_op jit(solution)/shard_map/ppermute | solution.py:61
  190.4 6.7 %shard_map.107.refs_10_ = f32[231,8192]{1,0:T(8,128)} custom-call(s32[9]{0:T(128)S(1)} %stack.269.order_ref, bf16[231,256]{1,0:T(8,128)(2,1)} %get-tuple-element.71.lo_ref, bf16[231,256]{1,0:T(8,128)(2,1)} %copy-done.4, f32[231,8192]{1,0:T(8,128)} %m_ref.3, bf16[231,8192]{1,0:T(8,128)(2,1)} %g_ref.3, bf16[4,288,512]{2,1,0:T(8,128)(2,1)S(1)} %pad_maximum_fusion.refs_0_, ...), custom_call_target="tpu_custom_call" | custom-call | tf_op jit(solution)/shard_map/pallas_call | solution.py:393
  200.7 11.5 %shard_map.109 = (f32[231,8192]{1,0:T(8,128)}, bf16[3696,512]{1,0:T(8,128)(2,1)}, bf16[64,512]{1,0:T(8,128)(2,1)}, bf16[64,512]{1,0:T(8,128)(2,1)}) custom-call(s32[7]{0:T(128)S(1)} %stack.227.order_ref, bf16[231,256]{1,0:T(8,128)(2,1)} %get-tuple-element.71.lo_ref, bf16[231,256]{1,0:T(8,128)(2,1)} %copy-done.4, ...), custom_call_target="tpu_custom_call", output_to_operand_aliasing={{0}: (15, {})} | custom-call | tf_op jit(solution)/shard_map/pallas_call | solution.py:393
  (169 shorter events, 76.3 us)
Async XLA Ops:
  7.2 46.2 %all-gather.4.cloned.1.call-start = ((), (), s32[]{:S(2)}) async-start(), calls=%async_computation | async-start | bytes 4276224 | tf_op jit(solution)/shard_map/all_gather | solution.py:481
  9.5 12.3 %collective-permute-start.4 = (bf16[32,3696]{1,0:T(8,128)(2,1)}, bf16[32,3696]{1,0:T(8,128)(2,1)S(1)}, u32[]{:S(2)}, u32[]{:S(2)}) collective-permute-start(bf16[32,3696]{1,0:T(8,128)(2,1)} %param.11), channel_id=1, source_target_pairs={{0,8},{1,9},{2,10},{3,11},{4,12},{5,13},{6,14},{7,15},{16,24},{17,... | collective-permute-start | bytes 709640 | tf_op jit(solution)/shard_map/ppermute | solution.py:39
  22.8 144.8 %all-gather.6.cloned.1.call-start = ((), (), s32[]{:S(2)}) async-start(), calls=%async_computation.1 | async-start | bytes 2365440 | tf_op jit(solution)/shard_map/all_gather | solution.py:44
  22.8 12.1 %collective-permute-start.7 = (bf16[512,256]{1,0:T(8,128)(2,1)S(1)}, bf16[512,256]{1,0:T(8,128)(2,1)S(1)}, u32[]{:S(2)}, u32[]{:S(2)}) collective-permute-start(bf16[512,256]{1,0:T(8,128)(2,1)S(1)} %bitcast.138), channel_id=1, source_target_pairs={{0,16},{1,33},{2,18},{3,35},{4,20},{5,37},{6,22},{7,39},{16,8},{17... | collective-permute-start | bytes 786440 | tf_op jit(solution)/shard_map/ppermute | solution.py:39
  24.1 10.8 %collective-permute-start.6 = (bf16[512,256]{1,0:T(8,128)(2,1)S(1)}, bf16[512,256]{1,0:T(8,128)(2,1)S(1)}, u32[]{:S(2)}, u32[]{:S(2)}) collective-permute-start(bf16[512,256]{1,0:T(8,128)(2,1)S(1)} %bitcast.139), channel_id=1, source_target_pairs={{0,8},{1,65},{2,10},{3,67},{4,12},{5,69},{6,14},{7,71},{16,24},{17... | collective-permute-start | bytes 786440 | tf_op jit(solution)/shard_map/ppermute | solution.py:39
  35.1 27.0 %collective-permute-start.8 = (bf16[231,8192]{1,0:T(8,128)(2,1)}, bf16[231,8192]{1,0:T(8,128)(2,1)}, u32[]{:S(2)}, u32[]{:S(2)}) collective-permute-start(bf16[231,8192]{1,0:T(8,128)(2,1)} %add_convert_fusion.refs_0_.refs_1_.refs_2_.refs_3_), channel_id=1, source_target_pairs={{0,1},{1,0},{2,3},{3,2},{4,5},{5,4},{6,7},{7,6},{8,9},{9,8},{10,11... | collective-permute-start | bytes 11354120 | tf_op jit(solution)/shard_map/ppermute | solution.py:61
  36.4 24.5 %collective-permute-start.11 = (bf16[4,512,256]{2,1,0:T(8,128)(2,1)S(1)}, bf16[4,512,256]{2,1,0:T(8,128)(2,1)S(1)}, u32[]{:S(2)}, u32[]{:S(2)}) collective-permute-start(bf16[4,512,256]{2,1,0:T(8,128)(2,1)S(1)} %pad_maximum_fusion.1.refs_8_), channel_id=1, source_target_pairs={{0,32},{1,17},{2,34},{3,19},{4,36},{5,21},{6,38},{7,23},{16,48},{1... | collective-permute-start | bytes 3145736 | tf_op jit(solution)/shard_map/ppermute | solution.py:39
  36.6 25.5 %collective-permute-start.10 = (bf16[4,512,256]{2,1,0:T(8,128)(2,1)S(1)}, bf16[4,512,256]{2,1,0:T(8,128)(2,1)}, u32[]{:S(2)}, u32[]{:S(2)}) collective-permute-start(bf16[4,512,256]{2,1,0:T(8,128)(2,1)S(1)} %pad_maximum_fusion.1.refs_8_), channel_id=1, source_target_pairs={{0,96},{1,25},{2,98},{3,27},{4,100},{5,29},{6,102},{7,31},{16,112}... | collective-permute-start | bytes 3145736 | tf_op jit(solution)/shard_map/ppermute | solution.py:39
  39.1 28.9 %collective-permute-start.9 = (bf16[4,512,256]{2,1,0:T(8,128)(2,1)S(1)}, bf16[4,512,256]{2,1,0:T(8,128)(2,1)S(1)}, u32[]{:S(2)}, u32[]{:S(2)}) collective-permute-start(bf16[4,512,256]{2,1,0:T(8,128)(2,1)S(1)} %pad_maximum_fusion.1.refs_8_), channel_id=1, source_target_pairs={{0,64},{1,9},{2,66},{3,11},{4,68},{5,13},{6,70},{7,15},{16,80},{17... | collective-permute-start | bytes 3145736 | tf_op jit(solution)/shard_map/ppermute | solution.py:39
  74.0 34.5 %collective-permute-start.12 = (bf16[4,288,512]{2,1,0:T(8,128)(2,1)S(1)}, bf16[4,288,512]{2,1,0:T(8,128)(2,1)}, u32[]{:S(2)}, u32[]{:S(2)}) collective-permute-start(bf16[4,288,512]{2,1,0:T(8,128)(2,1)S(1)} %shard_map.104), channel_id=1, source_target_pairs={{0,64},{1,9},{2,66},{3,11},{4,68},{5,13},{6,70},{7,15},{16,80},{17... | collective-permute-start | bytes 3538952 | tf_op jit(solution)/shard_map/ppermute | solution.py:39
  81.0 27.5 %collective-permute-start.15 = (bf16[4,288,512]{2,1,0:T(8,128)(2,1)}, bf16[4,288,512]{2,1,0:T(8,128)(2,1)}, u32[]{:S(2)}, u32[]{:S(2)}) collective-permute-start(bf16[4,288,512]{2,1,0:T(8,128)(2,1)} %get-tuple-element.63), channel_id=1, source_target_pairs={{0,96},{1,25},{2,98},{3,27},{4,100},{5,29},{6,102},{7,31},{16,112}... | collective-permute-start | bytes 3538952 | tf_op jit(solution)/shard_map/ppermute | solution.py:39
  82.8 25.7 %collective-permute-start.14 = (bf16[4,288,512]{2,1,0:T(8,128)(2,1)}, bf16[4,288,512]{2,1,0:T(8,128)(2,1)}, u32[]{:S(2)}, u32[]{:S(2)}) collective-permute-start(bf16[4,288,512]{2,1,0:T(8,128)(2,1)} %get-tuple-element.60), channel_id=1, source_target_pairs={{0,32},{1,17},{2,34},{3,19},{4,36},{5,21},{6,38},{7,23},{16,48},{1... | collective-permute-start | bytes 3538952 | tf_op jit(solution)/shard_map/ppermute | solution.py:39
  83.6 24.8 %collective-permute-start.13 = (bf16[2,231,256]{2,1,0:T(8,128)(2,1)S(1)}, bf16[2,231,256]{2,1,0:T(8,128)(2,1)S(1)}, u32[]{:S(2)}, u32[]{:S(2)}) collective-permute-start(bf16[2,231,256]{2,1,0:T(8,128)(2,1)S(1)} %pad_maximum_fusion.4), channel_id=1, source_target_pairs={{0,8},{1,9},{2,10},{3,11},{4,12},{5,13},{6,14},{7,15},{16,24},{17,... | collective-permute-start | bytes 709640 | tf_op jit(solution)/shard_map/ppermute | solution.py:39
  126.6 9.8 %collective-permute-start.22 = (bf16[288,128]{0,1:T(8,128)(2,1)S(1)}, bf16[288,128]{0,1:T(8,128)(2,1)S(1)}, u32[]{:S(2)}, u32[]{:S(2)}) collective-permute-start(bf16[288,128]{0,1:T(8,128)(2,1)S(1)} %get-tuple-element.100), channel_id=1, source_target_pairs={{0,2},{1,3},{2,4},{3,5},{4,6},{5,7},{6,0},{7,1},{16,18},{17,19},{1... | collective-permute-start | bytes 221192 | tf_op jit(solution)/shard_map/ppermute | solution.py:39
  127.3 9.3 %collective-permute-start.23 = (bf16[288,128]{0,1:T(8,128)(2,1)S(1)}, bf16[288,128]{0,1:T(8,128)(2,1)S(1)}, u32[]{:S(2)}, u32[]{:S(2)}) collective-permute-start(bf16[288,128]{0,1:T(8,128)(2,1)S(1)} %get-tuple-element.101), channel_id=1, source_target_pairs={{0,6},{1,7},{2,0},{3,1},{4,2},{5,3},{6,4},{7,5},{16,22},{17,23},{1... | collective-permute-start | bytes 221192 | tf_op jit(solution)/shard_map/ppermute | solution.py:39
  137.1 12.3 %collective-permute-start.26 = (bf16[288,128]{0,1:T(8,128)(2,1)S(1)}, bf16[288,128]{0,1:T(8,128)(2,1)S(1)}, u32[]{:S(2)}, u32[]{:S(2)}) collective-permute-start(bf16[288,128]{0,1:T(8,128)(2,1)S(1)} %get-tuple-element.87), channel_id=1, source_target_pairs={{0,2},{1,3},{2,4},{3,5},{4,6},{5,7},{6,0},{7,1},{16,18},{17,19},{1... | collective-permute-start | bytes 221192 | tf_op jit(solution)/shard_map/ppermute | solution.py:39
  137.8 11.5 %collective-permute-start.25 = (bf16[288,128]{0,1:T(8,128)(2,1)S(1)}, bf16[288,128]{0,1:T(8,128)(2,1)S(1)}, u32[]{:S(2)}, u32[]{:S(2)}) collective-permute-start(bf16[288,128]{0,1:T(8,128)(2,1)S(1)} %get-tuple-element.87), channel_id=1, source_target_pairs={{0,4},{1,5},{2,6},{3,7},{4,0},{5,1},{6,2},{7,3},{16,20},{17,21},{1... | collective-permute-start | bytes 221192 | tf_op jit(solution)/shard_map/ppermute | solution.py:39
  150.8 9.6 %collective-permute-start.30 = (bf16[288,512]{1,0:T(8,128)(2,1)S(1)}, bf16[288,512]{1,0:T(8,128)(2,1)S(1)}, u32[]{:S(2)}, u32[]{:S(2)}) collective-permute-start(bf16[288,512]{1,0:T(8,128)(2,1)S(1)} %copy.49), channel_id=1, source_target_pairs={{0,8},{1,65},{2,10},{3,67},{4,12},{5,69},{6,14},{7,71},{16,24},{17... | collective-permute-start | bytes 884744 | tf_op jit(solution)/shard_map/ppermute | solution.py:39
  161.5 15.7 %collective-permute-start.32 = (bf16[4,288,512]{2,1,0:T(8,128)(2,1)S(1)}, bf16[4,288,512]{2,1,0:T(8,128)(2,1)S(1)}, u32[]{:S(2)}, u32[]{:S(2)}) collective-permute-start(bf16[4,288,512]{2,1,0:T(8,128)(2,1)S(1)} %pad_maximum_fusion.refs_0_), channel_id=1, source_target_pairs={{0,96},{1,25},{2,98},{3,27},{4,100},{5,29},{6,102},{7,31},{16,112}... | collective-permute-start | bytes 3538952 | tf_op jit(solution)/shard_map/ppermute | solution.py:39
  164.0 16.6 %collective-permute-start.35 = (bf16[4,288,512]{2,1,0:T(8,128)(2,1)S(1)}, bf16[4,288,512]{2,1,0:T(8,128)(2,1)S(1)}, u32[]{:S(2)}, u32[]{:S(2)}) collective-permute-start(bf16[4,288,512]{2,1,0:T(8,128)(2,1)S(1)} %pad_maximum_fusion.refs_0_), channel_id=1, source_target_pairs={{0,32},{1,17},{2,34},{3,19},{4,36},{5,21},{6,38},{7,23},{16,48},{1... | collective-permute-start | bytes 3538952 | tf_op jit(solution)/shard_map/ppermute | solution.py:39
  164.0 24.3 %collective-permute-start.37 = (bf16[4,288,512]{2,1,0:T(8,128)(2,1)S(1)}, bf16[4,288,512]{2,1,0:T(8,128)(2,1)}, u32[]{:S(2)}, u32[]{:S(2)}) collective-permute-start(bf16[4,288,512]{2,1,0:T(8,128)(2,1)S(1)} %pad_maximum_fusion.refs_0_), channel_id=1, source_target_pairs={{0,1},{1,0},{2,3},{3,2},{4,5},{5,4},{6,7},{7,6},{8,9},{9,8},{10,11... | collective-permute-start | bytes 3538952 | tf_op jit(solution)/shard_map/ppermute | solution.py:61
  180.6 9.8 %collective-permute-start.39 = (bf16[4,288,512]{2,1,0:T(8,128)(2,1)S(1)}, bf16[4,288,512]{2,1,0:T(8,128)(2,1)}, u32[]{:S(2)}, u32[]{:S(2)}) collective-permute-start(bf16[4,288,512]{2,1,0:T(8,128)(2,1)S(1)} %collective-permute-done.35.refs_2_.refs_4_), channel_id=1, source_target_pairs={{0,1},{1,0},{2,3},{3,2},{4,5},{5,4},{6,7},{7,6},{8,9},{9,8},{10,11... | collective-permute-start | bytes 3538952 | tf_op jit(solution)/shard_map/ppermute | solution.py:61
  184.4 16.3 %collective-permute-start.43 = (bf16[3696,256]{1,0:T(8,128)(2,1)}, bf16[3696,256]{1,0:T(8,128)(2,1)}, u32[]{:S(2)}, u32[]{:S(2)}) collective-permute-start(bf16[3696,256]{1,0:T(8,128)(2,1)} %reshape.154.refs_17_), channel_id=1, source_target_pairs={{0,1},{1,0},{2,3},{3,2},{4,5},{5,4},{6,7},{7,6},{8,9},{9,8},{10,11... | collective-permute-start | bytes 5677064 | tf_op jit(solution)/shard_map/ppermute | solution.py:61
  186.6 10.6 %collective-permute-start.36 = (bf16[2,288,512]{2,1,0:T(8,128)(2,1)}, bf16[2,288,512]{2,1,0:T(8,128)(2,1)}, u32[]{:S(2)}, u32[]{:S(2)}) collective-permute-start(bf16[2,288,512]{2,1,0:T(8,128)(2,1)} %slice.131), channel_id=1, source_target_pairs={{0,32},{1,17},{2,34},{3,19},{4,36},{5,21},{6,38},{7,23},{16,48},{1... | collective-permute-start | bytes 1769480 | tf_op jit(solution)/shard_map/ppermute | solution.py:39
  (29 other events, 191.5 us)
Sparse Core Ops, SparseCore 0:
  22.9 30.4 all-gather.3
  113.5 37.1 all-gather.5
